TPU v7x, 512 devices: a whole 4x8x8 slice. The times are simulated.
512 devices in a mesh: lat: 16 (over z, core), tgt: 16 (over x_lo, y), tok: 2 (over x_hi).
Axes of the slice: x: 4 (x_hi: 2, x_lo: 2; x = x_hi * 2 + x_lo), y: 8, z: 8, core: 2. Of those that a mesh axis runs over, the one named last changes fastest.
Arguments:
- errors: bfloat16 [16, 2048, 4096], P('tgt', 'tok', 'lat'), may hold values from -6 to 6
- decoder: bfloat16 [16, 4096, 4096], P('tgt', 'lat'), may hold values from -0.0234375 to 0.0234375
- pre_acts: bfloat16 [2048, 4096], P('tok', 'lat'), may hold values from -0.796875 to 0.796875
- inputs: bfloat16 [2048, 4096], P('tok', 'tgt'), may hold values from -0.796875 to 0.796875
- encoder: bfloat16 [4096, 4096], P('tgt', 'lat'), may hold values from -0.1875 to 0.1875
- block_mask: int32 [16, 32], P('tok', 'lat'), may hold values from 0 to 1, as said below
Outputs:
- dec_grad: bfloat16 [16, 4096, 4096], P('tgt', 'lat', 'tok')
- enc_grad: float32 [4096, 4096], P(('tgt', 'tok'), 'lat')
- input_grad: bfloat16 [2048, 4096], P('tok', 'tgt')
Inputs may be any that keep to these rules, and one draw needn't show every extreme that they name: `block_mask`: 1 marks an active block of 128 tokens by 128 latents, 0 an inactive one.
All inputs are finite; a program needn't handle non-finite values.
Results may differ from a plain program's by a relative error of at most 0.0051.
Values may be sent and summed in bfloat16 or wider, within the bound.
No kernel may reach another device: no remote copies, remote signals or barrier semaphores. Data moves between devices by JAX's collectives and lax.ppermute only.
A program may use at most 64 MiB of HBM per device.

v0:
```python
import jax
import jax.numpy as jnp
from jax import lax
from jax.sharding import PartitionSpec as P


def expand_mask(block_mask, block):
    return jnp.repeat(jnp.repeat(block_mask, block, axis=0), block, axis=1)


def rounded(value):
    return lax.optimization_barrier(value.astype(jnp.bfloat16)).astype(jnp.float32)


def dense_products(whole, weights, latents):
    grad_part = lax.dot_general(
        whole, weights, (((1,), (1,)), ((), ())), preferred_element_type=jnp.float32
    )
    dec_part = lax.dot_general(
        latents, whole, (((0,), (0,)), ((), ())), preferred_element_type=jnp.float32
    )
    return (grad_part, dec_part)


def shards(errors, decoder, pre_acts, inputs, encoder, block_mask):
    block = pre_acts.shape[0] // block_mask.shape[0]
    live = (expand_mask(block_mask, block) > 0) & (pre_acts > 0)
    latents = jnp.where(live, pre_acts, jnp.zeros_like(pre_acts))
    whole = lax.all_gather(errors[0], "lat", axis=1, tiled=True)
    weights = decoder[0]
    grad_part, dec_part = dense_products(whole, weights, latents)
    dec_total = lax.psum_scatter(
        rounded(dec_part).astype(jnp.bfloat16), "tok", scatter_dimension=1, tiled=True
    )
    dec_layers = [dec_total]
    dec_grad = jnp.stack(dec_layers)
    total = lax.psum(grad_part, "tgt")
    delta = jnp.where(live, total, jnp.zeros_like(total)).astype(jnp.bfloat16)
    enc_part = lax.dot_general(
        inputs, delta, (((0,), (0,)), ((), ())), preferred_element_type=jnp.float32
    )
    enc_grad = lax.psum_scatter(enc_part, "tok", scatter_dimension=0, tiled=True)
    input_part = lax.dot_general(
        delta, encoder, (((1,), (1,)), ((), ())), preferred_element_type=jnp.float32
    )
    input_grad = lax.psum(input_part, "lat").astype(jnp.bfloat16)
    return (dec_grad, enc_grad, input_grad)


def solution(mesh):
    in_specs = (
        P("tgt", "tok", "lat"),
        P("tgt", "lat", None),
        P("tok", "lat"),
        P("tok", "tgt"),
        P("tgt", "lat"),
        P("tok", "lat"),
    )
    out_specs = (P("tgt", "lat", "tok"), P(("tgt", "tok"), "lat"), P("tok", "tgt"))
    return jax.shard_map(shards, mesh=mesh, in_specs=in_specs, out_specs=out_specs, check_vma=False)
```

profile of v0, /device:TPU:1, one launch (start us, length us, event | category | flops | bytes accessed | tf_op | source)
XLA Modules:
  0.0 243.2 jit_solution(8942176679790094444)
XLA Ops:
  7.2 0.0 copy-start
  7.2 0.0 all-gather.3.cloned.1.call-start
  7.2 0.7 all-gather.3.cloned.1.call-update
  7.9 0.0 reduce-scatter.5.cloned.1.call-start
  8.0 0.7 broadcast_compare_fusion
  8.6 0.1 broadcast_bitcast_fusion
  8.7 0.1 broadcast_in_dim.10
  8.8 0.4 copy.11
  9.2 0.0 copy-start.1
  9.2 76.1 %all-gather.3.cloned.1.call-done = bf16[1,1024,4096]{2,1,0:T(8,128)(2,1)} async-done(((bf16[1,1024,256]{2,1,0:T(8,128)(2,1)}), bf16[1,1024,4096]{2,1,0:T(8,128)(2,1)}) %all-gather.3.cloned.1.call-update) | async-done | bytes 8388624 | tf_op jit(solution)/shard_map/all_gather | solution.py:29
  85.3 0.0 copy-done
  85.3 6.7 %fusion = f32[1024,256]{1,0:T(8,128)} fusion(bf16[1,1024,4096]{2,1,0:T(8,128)(2,1)} %all-gather.3.cloned.1.call-done, bf16[1,256,4096]{2,1,0:T(8,128)(2,1)S(1)} %copy-done), kind=kOutput, calls=%fused_computation | convolution fusion | flops 2147483648 | bytes 11534336 | tf_op jit(solution)/shard_map/dot_general | solution.py:16
  92.0 60.9 %all-reduce.2 = bf16[1024,256]{1,0:T(8,128)(2,1)} all-reduce(f32[1024,256]{1,0:T(8,128)} %fusion), channel_id=1, replica_groups=mesh['lat'=16,'tgt'=16,'tok'=2] {'tgt'}, use_global_device_ids=true, to_apply=%region_1.2 | all-reduce | flops 262144 | bytes 1572864 | tf_op jit(solution)/shard_map/psum | solution.py:37
  152.9 0.0 copy-done.1
  153.0 1.3 select_convert_fusion
  154.3 2.1 convolution_bitcast_fusion
  156.4 0.0 reduce-scatter.5.cloned.1.call-update
  156.4 0.0 copy-start.2
  156.4 0.0 reduce-scatter.3.cloned.1.call-start
  156.5 7.3 %fusion.4 = bf16[256,4096]{1,0:T(8,128)(2,1)} fusion(bf16[1,1024,4096]{2,1,0:T(8,128)(2,1)} %all-gather.3.cloned.1.call-done, bf16[1024,256]{1,0:T(8,128)(2,1)S(1)} %copy-done.1, pred[1024,256]{1,0:T(32,128)(4,1)S(1)} %copy.11), kind=kOutput, calls=%fused_computation.4 | convolution fusion | flops 2149842944 | bytes 11272192 | tf_op jit(solution)/shard_map/dot_general | solution.py:19
  163.8 0.0 reduce-scatter.3.cloned.1.call-update
  163.8 1.3 fusion.12
  165.1 69.8 %all-reduce.3 = bf16[1024,256]{1,0:T(8,128)(2,1)} all-reduce(f32[1024,256]{1,0:T(8,128)} %fusion.12), channel_id=1, replica_groups=mesh['lat'=16,'tgt'=16,'tok'=2] {'lat'}, use_global_device_ids=true, to_apply=%region_3.4 | all-reduce | flops 262144 | bytes 1572864 | tf_op jit(solution)/shard_map/psum | solution.py:46
  235.0 1.7 copy.12
  (4 shorter events, 0.0 us)
Async XLA Ops:
  7.2 78.1 %copy-start = (bf16[1,256,4096]{2,1,0:T(8,128)(2,1)S(1)}, bf16[1,256,4096]{2,1,0:T(8,128)(2,1)}, u32[]{:S(2)}) copy-start(bf16[1,256,4096]{2,1,0:T(8,128)(2,1)} %param.7) | copy-start | bytes 6291460
  7.2 78.1 %all-gather.3.cloned.1.call-start = ((), (), s32[]{:S(2)}) async-start(), calls=%async_computation.4 | async-start | bytes 8912896 | tf_op jit(solution)/shard_map/all_gather | solution.py:29
  7.9 227.0 %reduce-scatter.5.cloned.1.call-start = ((), (), s32[]{:S(2)}) async-start(), calls=%async_computation.3 | async-start | bytes 393216 | tf_op jit(solution)/shard_map/reduce_scatter | solution.py:42
  9.2 143.8 %copy-start.1 = (bf16[1024,256]{1,0:T(8,128)(2,1)S(1)}, bf16[1024,256]{1,0:T(8,128)(2,1)}, u32[]{:S(2)}) copy-start(bf16[1024,256]{1,0:T(8,128)(2,1)} %param.8) | copy-start | bytes 1572868
  156.4 7.4 %copy-start.2 = (bf16[256,256]{1,0:T(8,128)(2,1)S(1)}, bf16[256,256]{1,0:T(8,128)(2,1)}, u32[]{:S(2)}) copy-start(bf16[256,256]{1,0:T(8,128)(2,1)} %param.10) | copy-start | bytes 393220
  156.4 80.2 %reduce-scatter.3.cloned.1.call-start = ((), (), s32[]{:S(2)}) async-start(), calls=%async_computation.2 | async-start | bytes 3145728 | tf_op jit(solution)/shard_map/reduce_scatter | solution.py:32
Sparse Core Ops, SparseCore 0:
  10.1 75.1 all-gather.2
  156.5 28.5 reduce-scatter.4
  188.7 40.7 reduce-scatter.2
where the time goes:
time: 246 us; the launch traced here: 243 us
  blocking collectives  131 us (53%)
  waiting for transfers between devices  76.8 us (31%)
  matrix products  17.4 us (7%)
  between operations  13.8 us (6%)
    all_gather x1, waiting for transfers between devices, shards(): whole = lax.all_gather(errors[0], 'lat', axis=1, tiled=True)  76.1 us
    psum x1, blocking collectives, shards(): input_grad = lax.psum(input_part, 'lat').astype(jnp.bfloat16)  69.8 us
    psum x1, blocking collectives, shards(): total = lax.psum(grad_part, 'tgt')  60.9 us
    dot_general x1, matrix products, dense_products(): lax.dot_general(latents, whole, (((0,), (0,)), ((), ())), preferred_eleme...  7.28 us
    dot_general x1, matrix products, dense_products(): lax.dot_general(whole, weights, (((1,), (1,)), ((), ())), preferred_eleme...  6.72 us
  transfers between devices with their start and end apart: 3, of which 1 were waited for; matrix products, arithmetic and copies ran while one was open for 5% of the time, Pallas kernels for 0%

commit v1 on v0

v1 whole, which is shorter than its diff:
```python
import functools

import jax
import jax.numpy as jnp
from jax import lax
from jax.experimental import pallas as pl
from jax.experimental.pallas import tpu as pltpu
from jax.sharding import PartitionSpec as P

F32 = jnp.float32
BF16 = jnp.bfloat16


def products_kernel(err_ref, dec_ref, lat_t_ref, live_ref, grad_ref, part_ref, total):
    step = pl.program_id(0)
    err = err_ref[0]
    term = lax.dot_general(err, dec_ref[...], (((1,), (1,)), ((), ())), preferred_element_type=F32)

    @pl.when(step == 0)
    def _():
        total[...] = term

    @pl.when(step > 0)
    def _():
        total[...] += term

    part_ref[...] = jnp.dot(lat_t_ref[...], err, preferred_element_type=F32).astype(BF16)

    @pl.when(step == pl.num_programs(0) - 1)
    def _():
        grad_ref[...] = jnp.where(live_ref[...] > 0, total[...], 0.0).astype(BF16)


def products(whole, weights, lat_t, latents):
    n, tokens, width = whole.shape
    rows = weights.shape[0]
    return pl.pallas_call(
        products_kernel,
        grid=(n,),
        in_specs=[
            pl.BlockSpec((1, tokens, width), lambda i: (i, 0, 0)),
            pl.BlockSpec((rows, width), lambda i: (0, i)),
            pl.BlockSpec((rows, tokens), lambda i: (0, 0)),
            pl.BlockSpec((tokens, rows), lambda i: (0, 0)),
        ],
        out_specs=[
            pl.BlockSpec((tokens, rows), lambda i: (0, 0)),
            pl.BlockSpec((rows, width), lambda i: (0, i)),
        ],
        out_shape=[
            jax.ShapeDtypeStruct((tokens, rows), BF16),
            jax.ShapeDtypeStruct((rows, n * width), BF16),
        ],
        scratch_shapes=[pltpu.VMEM((tokens, rows), F32)],
        compiler_params=pltpu.CompilerParams(vmem_limit_bytes=32 * 1024 * 1024),
        cost_estimate=pl.CostEstimate(
            flops=4 * n * tokens * width * rows,
            bytes_accessed=2 * n * tokens * width + 4 * rows * n * width,
            transcendentals=0,
        ),
    )(whole, weights, lat_t, latents)


def scatter_sum(terms, axis):
    n = lax.axis_size(axis)
    got = lax.all_to_all(terms.reshape(n, terms.shape[0] // n, terms.shape[1]), axis, 0, 0)
    return jnp.sum(got.astype(F32), axis=0)


def gather(chunk, axis):
    n = lax.axis_size(axis)
    got = lax.all_to_all(jnp.broadcast_to(chunk[None], (n,) + chunk.shape), axis, 0, 0)
    return got.reshape(n * chunk.shape[0], chunk.shape[1])


def shards(errors, decoder, pre_acts, inputs, encoder, block_mask):
    block = pre_acts.shape[0] // block_mask.shape[0]
    cells = jnp.repeat(jnp.repeat(block_mask, block, axis=0), block, axis=1)
    live = (cells > 0) & (pre_acts > 0)
    latents = jnp.where(live, pre_acts, jnp.zeros_like(pre_acts))
    whole = lax.all_gather(errors[0], "lat", axis=0, tiled=False)
    grad_part, dec_part = products(whole, decoder[0], latents.T, latents)
    half = dec_part.shape[1] // 2
    mine = lax.axis_index("tok")
    keep = lax.dynamic_slice_in_dim(dec_part, mine * half, half, 1)
    send = lax.dynamic_slice_in_dim(dec_part, (1 - mine) * half, half, 1)
    other = lax.ppermute(send, "tok", [(0, 1), (1, 0)])
    dec_grad = (keep.astype(F32) + other.astype(F32)).astype(BF16)[None]

    delta_chunk = scatter_sum(grad_part, "tgt").astype(BF16)
    delta = gather(delta_chunk, "tgt")
    enc_part = lax.dot_general(inputs, delta, (((0,), (0,)), ((), ())), preferred_element_type=F32)
    rows = enc_part.shape[0] // 2
    enc_keep = lax.dynamic_slice_in_dim(enc_part, mine * rows, rows, 0)
    enc_send = lax.dynamic_slice_in_dim(enc_part, (1 - mine) * rows, rows, 0)
    enc_grad = enc_keep + lax.ppermute(enc_send, "tok", [(0, 1), (1, 0)])

    input_part = lax.dot_general(delta, encoder, (((1,), (1,)), ((), ())), preferred_element_type=F32)
    input_grad = gather(scatter_sum(input_part.astype(BF16), "lat").astype(BF16), "lat")
    return (dec_grad, enc_grad, input_grad)


def solution(mesh):
    in_specs = (
        P("tgt", "tok", "lat"),
        P("tgt", "lat", None),
        P("tok", "lat"),
        P("tok", "tgt"),
        P("tgt", "lat"),
        P("tok", "lat"),
    )
    out_specs = (P("tgt", "lat", "tok"), P(("tgt", "tok"), "lat"), P("tok", "tgt"))
    return jax.shard_map(shards, mesh=mesh, in_specs=in_specs, out_specs=out_specs, check_vma=False)
```

time: 246 us -> 196 us (0.80)
  blocking collectives: 131 us -> 40.8 us
  starting transfers between devices: 0.12 us -> 20 us
  Pallas kernels: 0 us -> 16.2 us
  matrix products: 17.4 us -> 1.46 us
  local copies, waits for them, and re-layouts: 2.19 us -> 12.2 us
  waiting for transfers between devices: 76.8 us -> 84.6 us
  other arithmetic: 2.02 us -> 5.99 us
    psum x2 -> x0, blocking collectives: 131 us -> none  [the longest x1 69.8 us: shards(): input_grad = lax.psum(input_part, 'lat').astype(jnp.bfloat16)]
    all_to_all x0 -> x2, blocking collectives: none -> 40.8 us  [the longest x1 21 us: scatter_sum(): lax.all_to_all(terms.reshape(n, terms.shape[0] // n, terms.shape[1]), axi...]
    all_to_all x0 -> x2, waiting for transfers between devices: none -> 18.3 us  [the longest x1 12.1 us: scatter_sum(): lax.all_to_all(terms.reshape(n, terms.shape[0] // n, terms.shape[1]), axi...]
    pallas_call x0 -> x1, Pallas kernels: none -> 16.2 us  [products(): pl.pallas_call(products_kernel, grid=(n,), in_specs=[pl.BlockSpec((1, tok...]
    dot_general x2 -> x0, matrix products: 14 us -> none  [the longest x1 7.28 us: dense_products(): lax.dot_general(latents, whole, (((0,), (0,)), ((), ())), preferred_eleme...]
    all_gather x1, waiting for transfers between devices: 76.1 us -> 63.7 us  [shards(): whole = lax.all_gather(errors[0], 'lat', axis=0, tiled=False)]
    all_to_all x0 -> x2, starting transfers between devices: none -> 11.4 us  [the longest x1 7.24 us: scatter_sum(): lax.all_to_all(terms.reshape(n, terms.shape[0] // n, terms.shape[1]), axi...]
    ppermute x0 -> x2, starting transfers between devices: none -> 8.61 us  [the longest x1 4.31 us: shards(): enc_grad = enc_keep + lax.ppermute(enc_send, 'tok', [(0, 1), (1, 0)])]
  transfers between devices with their start and end apart: 3 -> 5, of which waited for: 1 -> 5; matrix products, arithmetic and copies ran while one was open for 5% -> 5% of each run, Pallas kernels for 0% -> 0%
where the time goes in v1:
time: 196 us; the launch traced here: 195 us
  waiting for transfers between devices  84.6 us (43%)
  blocking collectives  40.8 us (21%)
  starting transfers between devices  20 us (10%)
  Pallas kernels  16.2 us (8%)
  between operations  14.1 us (7%)
  local copies, waits for them, and re-layouts  12.2 us (6%)
  other arithmetic  5.99 us (3%)
    all_gather x1, waiting for transfers between devices, shards(): whole = lax.all_gather(errors[0], 'lat', axis=0, tiled=False)  63.7 us
    all_to_all x1, blocking collectives, scatter_sum(): lax.all_to_all(terms.reshape(n, terms.shape[0] // n, terms.shape[1]), axi...  21 us
    all_to_all x1, blocking collectives, gather(): lax.all_to_all(jnp.broadcast_to(chunk[None], (n,) + chunk.shape), axis, 0...  19.8 us
    pallas_call x1, Pallas kernels, products(): pl.pallas_call(products_kernel, grid=(n,), in_specs=[pl.BlockSpec((1, tok...  16.2 us
    all_to_all x1, waiting for transfers between devices, scatter_sum(): lax.all_to_all(terms.reshape(n, terms.shape[0] // n, terms.shape[1]), axi...  12.1 us
    unnamed x14, local copies, waits for them, and re-layouts  8.74 us
    all_to_all x1, starting transfers between devices, scatter_sum(): lax.all_to_all(terms.reshape(n, terms.shape[0] // n, terms.shape[1]), axi...  7.24 us
    all_to_all x1, waiting for transfers between devices, gather(): lax.all_to_all(jnp.broadcast_to(chunk[None], (n,) + chunk.shape), axis, 0...  6.2 us
  transfers between devices with their start and end apart: 5, of which 5 were waited for; matrix products, arithmetic and copies ran while one was open for 5% of the time, Pallas kernels for 0%

profile of v1, /device:TPU:1, one launch (start us, length us, event | category | flops | bytes accessed | tf_op | source)
XLA Modules:
  0.0 195.5 jit_solution(14239706264073790199)
XLA Ops:
  9.2 1.5 and_select_fusion.live_ref
  10.7 1.0 copy.16.lat_t_ref
  11.7 63.7 %all-gather.2.cloned.1.call-done.err_ref = bf16[16,1024,256]{2,1,0:T(8,128)(2,1)} async-done(((bf16[1,1024,256]{2,1,0:T(8,128)(2,1)}), bf16[16,1024,256]{2,1,0:T(8,128)(2,1)}) %all-gather.2.cloned.1.call-update) | async-done | bytes 8388624 | tf_op jit(solution)/shard_map/all_gather | solution.py:81
  75.4 1.0 copy-done.1
  76.5 3.4 %copy-done.2 = bf16[16,1024,256]{2,1,0:T(8,128)(2,1)S(1)} copy-done((bf16[16,1024,256]{2,1,0:T(8,128)(2,1)S(1)}, bf16[16,1024,256]{2,1,0:T(8,128)(2,1)}, u32[]{:S(2)}) %copy-start.2) | copy-done | bytes 8388632
  79.8 1.6 copy-done.3
  81.4 16.2 %shard_map.85 = (bf16[1024,256]{1,0:T(8,128)(2,1)S(1)}, bf16[256,4096]{1,0:T(8,128)(2,1)S(1)}) custom-call(bf16[16,1024,256]{2,1,0:T(8,128)(2,1)S(1)} %copy-done.2, bf16[256,4096]{1,0:T(8,128)(2,1)S(1)} %bitcast.26, bf16[256,1024]{1,0:T(8,128)(2,1)S(1)} %copy-done.1, bf16[1024,256]{1,0:T(8,128)(2,1)S(1)} %and_select_fusion.live_ref), custom_call_target="tpu_custom_call" | custom-call | flops 4294967296 | bytes 12582912 | tf_op jit(solution)/shard_map/pallas_call | solution.py:37
  97.7 21.0 %all_to_all.20 = bf16[16,64,256]{2,1,0:T(8,128)(2,1)S(1)} all-to-all(bf16[16,64,256]{2,1,0:T(8,128)(2,1)S(1)} %bitcast.25), channel_id=1, replica_groups=mesh['lat'=16,'tgt'=16,'tok'=2] {'tgt'}, dimensions={0} | all-to-all | bytes 1048576 | tf_op jit(solution)/shard_map/all_to_all | solution.py:66
  118.9 19.8 %all_to_all.21 = bf16[16,64,256]{2,1,0:T(8,128)(2,1)S(1)} all-to-all(bf16[16,64,256]{2,1,0:T(8,128)(2,1)S(1)} %broadcast_in_dim.24), channel_id=1, replica_groups=mesh['lat'=16,'tgt'=16,'tok'=2] {'tgt'}, dimensions={0} | all-to-all | bytes 1048576 | tf_op jit(solution)/shard_map/all_to_all | solution.py:72
  138.7 1.1 convolution_convert_fusion
  139.8 7.2 %all-to-all-start.2 = ((bf16[16,64,256]{2,1,0:T(8,128)(2,1)}), bf16[16,64,256]{2,1,0:T(8,128)(2,1)}, u32[]{:S(2)}, u32[]{:S(2)}) async-start(bf16[16,64,256]{2,1,0:T(8,128)(2,1)} %bitcast.29), calls=%async_computation.2 | async-start | bytes 1048576 | tf_op jit(solution)/shard_map/all_to_all | solution.py:66
  147.0 1.0 constant_dynamic-slice_fusion
  148.1 4.3 %collective-permute-start = (bf16[256,2048]{1,0:T(8,128)(2,1)}, bf16[256,2048]{1,0:T(8,128)(2,1)}, u32[]{:S(2)}, u32[]{:S(2)}) collective-permute-start(bf16[256,2048]{1,0:T(8,128)(2,1)} %constant_dynamic-slice_fusion), channel_id=1, source_target_pairs={{0,1},{1,0},{2,3},{3,2},{4,5},{5,4},{6,7},{7,6},{8,9},{9,8},{10,11... | collective-permute-start | bytes 3145736 | tf_op jit(solution)/shard_map/ppermute | solution.py:87
  152.4 12.1 %all-to-all-done.2 = bf16[16,64,256]{2,1,0:T(8,128)(2,1)} async-done(((bf16[16,64,256]{2,1,0:T(8,128)(2,1)}), bf16[16,64,256]{2,1,0:T(8,128)(2,1)}, u32[]{:S(2)}, u32[]{:S(2)}) %all-to-all-start.2) | async-done | bytes 524320 | tf_op jit(solution)/shard_map/all_to_all | solution.py:66
  164.5 1.1 reduce_sum.25
  165.6 0.8 broadcast_in_dim.25
  166.4 4.1 %all-to-all-start.3 = ((bf16[16,64,256]{2,1,0:T(8,128)(2,1)}), bf16[16,64,256]{2,1,0:T(8,128)(2,1)}, u32[]{:S(2)}, u32[]{:S(2)}) async-start(bf16[16,64,256]{2,1,0:T(8,128)(2,1)} %broadcast_in_dim.25), calls=%async_computation.3 | async-start | bytes 1048576 | tf_op jit(solution)/shard_map/all_to_all | solution.py:72
  171.0 4.3 %collective-permute-start.1 = (f32[128,256]{0,1:T(8,128)S(1)}, f32[128,256]{0,1:T(8,128)S(1)}, u32[]{:S(2)}, u32[]{:S(2)}) collective-permute-start(f32[128,256]{0,1:T(8,128)S(1)} %dynamic-slice_bitcast_fusion), channel_id=1, source_target_pairs={{0,1},{1,0},{2,3},{3,2},{4,5},{5,4},{6,7},{7,6},{8,9},{9,8},{10,11... | collective-permute-start | bytes 393224 | tf_op jit(solution)/shard_map/ppermute | solution.py:96
  175.3 1.1 collective-permute-done
  176.4 2.6 %fusion = bf16[1,256,2048]{2,1,0:T(8,128)(2,1)} fusion(bf16[256,2048]{1,0:T(8,128)(2,1)} %collective-permute-done, bf16[256,4096]{1,0:T(8,128)(2,1)S(1)} %get-tuple-element.5, s32[]{:T(128)S(6)} %select_n.17), kind=kLoop, calls=%fused_computation.2 | loop fusion | flops 2097152 | bytes 3145732 | tf_op jit(solution)/shard_map/broadcast_in_dim | solution.py:88
  178.9 0.8 collective-permute-done.1
  179.8 0.8 copy.17
  180.6 6.2 %all-to-all-done.3 = bf16[16,64,256]{2,1,0:T(8,128)(2,1)} async-done(((bf16[16,64,256]{2,1,0:T(8,128)(2,1)}), bf16[16,64,256]{2,1,0:T(8,128)(2,1)}, u32[]{:S(2)}, u32[]{:S(2)}) %all-to-all-start.3) | async-done | bytes 524320 | tf_op jit(solution)/shard_map/all_to_all | solution.py:72
  186.8 1.9 copy.22
  (19 shorter events, 2.5 us)
Async XLA Ops:
  7.2 163.4 %copy-start = (bf16[1024,256]{1,0:T(8,128)(2,1)S(1)}, bf16[1024,256]{1,0:T(8,128)(2,1)}, u32[]{:S(2)}) copy-start(bf16[1024,256]{1,0:T(8,128)(2,1)} %param.9) | copy-start | bytes 1572868
  7.2 68.2 %all-gather.2.cloned.1.call-start = ((), (), s32[]{:S(2)}) async-start(), calls=%async_computation.4 | async-start | bytes 8912896 | tf_op jit(solution)/shard_map/all_gather | solution.py:81
  75.4 1.0 copy-start.1
  76.5 3.4 %copy-start.2 = (bf16[16,1024,256]{2,1,0:T(8,128)(2,1)S(1)}, bf16[16,1024,256]{2,1,0:T(8,128)(2,1)}, u32[]{:S(2)}) copy-start(bf16[16,1024,256]{2,1,0:T(8,128)(2,1)} %all-gather.2.cloned.1.call-done.err_ref) | copy-start | bytes 25165828
  79.8 1.6 copy-start.3
  97.7 41.0 %copy-start.4 = (bf16[256,256]{1,0:T(8,128)(2,1)S(1)}, bf16[256,256]{1,0:T(8,128)(2,1)}, u32[]{:S(2)}) copy-start(bf16[256,256]{1,0:T(8,128)(2,1)} %param.10) | copy-start | bytes 393220
  139.8 24.7 %all-to-all-start.2 = ((bf16[16,64,256]{2,1,0:T(8,128)(2,1)}), bf16[16,64,256]{2,1,0:T(8,128)(2,1)}, u32[]{:S(2)}, u32[]{:S(2)}) async-start(bf16[16,64,256]{2,1,0:T(8,128)(2,1)} %bitcast.29), calls=%async_computation.2 | async-start | bytes 1048576 | tf_op jit(solution)/shard_map/all_to_all | solution.py:66
  148.1 28.3 %collective-permute-start = (bf16[256,2048]{1,0:T(8,128)(2,1)}, bf16[256,2048]{1,0:T(8,128)(2,1)}, u32[]{:S(2)}, u32[]{:S(2)}) collective-permute-start(bf16[256,2048]{1,0:T(8,128)(2,1)} %constant_dynamic-slice_fusion), channel_id=1, source_target_pairs={{0,1},{1,0},{2,3},{3,2},{4,5},{5,4},{6,7},{7,6},{8,9},{9,8},{10,11... | collective-permute-start | bytes 3145736 | tf_op jit(solution)/shard_map/ppermute | solution.py:87
  166.4 20.3 %all-to-all-start.3 = ((bf16[16,64,256]{2,1,0:T(8,128)(2,1)}), bf16[16,64,256]{2,1,0:T(8,128)(2,1)}, u32[]{:S(2)}, u32[]{:S(2)}) async-start(bf16[16,64,256]{2,1,0:T(8,128)(2,1)} %broadcast_in_dim.25), calls=%async_computation.3 | async-start | bytes 1048576 | tf_op jit(solution)/shard_map/all_to_all | solution.py:72
  171.0 8.8 %collective-permute-start.1 = (f32[128,256]{0,1:T(8,128)S(1)}, f32[128,256]{0,1:T(8,128)S(1)}, u32[]{:S(2)}, u32[]{:S(2)}) collective-permute-start(f32[128,256]{0,1:T(8,128)S(1)} %dynamic-slice_bitcast_fusion), channel_id=1, source_target_pairs={{0,1},{1,0},{2,3},{3,2},{4,5},{5,4},{6,7},{7,6},{8,9},{9,8},{10,11... | collective-permute-start | bytes 393224 | tf_op jit(solution)/shard_map/ppermute | solution.py:96
Sparse Core Ops, SparseCore 0:
  10.1 65.2 all-gather.1

commit v2 on v0

v2 whole, which is shorter than its diff:
```python
import functools

import jax
import jax.numpy as jnp
from jax import lax
from jax.experimental import pallas as pl
from jax.experimental.pallas import tpu as pltpu
from jax.sharding import PartitionSpec as P

F32 = jnp.float32
BF16 = jnp.bfloat16
VMEM_BYTES = 20 * 1024 * 1024
COST = pl.CostEstimate(flops=1, bytes_accessed=1, transcendentals=0)
SMEM = pl.BlockSpec(memory_space=pltpu.SMEM)
VMEM = pl.BlockSpec(memory_space=pltpu.VMEM)


def nt(a, b):
    return lax.dot_general(a, b, (((1,), (1,)), ((), ())), preferred_element_type=F32)


def chunk_at(here, distance, nz):
    return lax.rem(here[0] + (2 * here[1] - 1) * distance + nz, nz)


def column(chunk, core, width):
    return pl.ds(pl.multiple_of((2 * chunk + core) * width, width), width)


def step_kernel(plan, distance, here, *refs):
    sibling, carried, carried_s, stacked = plan
    refs = list(refs)
    ex, ey, weights, lat_t = (refs.pop(0) for _ in range(4))
    if sibling:
        weights_s, lat_s = refs.pop(0), refs.pop(0)
    total_in = refs.pop(0) if carried else None
    total_s_in = refs.pop(0) if carried_s else None
    before = [refs.pop(0) for _ in range(stacked)]
    total, dec = refs.pop(0), refs.pop(0)
    n, width = lat_t.shape[0], ex.shape[1]
    chunk = chunk_at(here, distance, weights.shape[1] // (2 * width))
    at_x, at_y = column(chunk, here[1], width), column(chunk, 1 - here[1], width)
    x, y = ex[...], ey[...]
    term = nt(x, weights[:, at_x]) + nt(y, weights[:, at_y])
    total[...] = term + total_in[...] if carried else term
    dec[:n, :] = jnp.dot(lat_t[...], x, preferred_element_type=F32).astype(BF16)
    dec[n:, :] = jnp.dot(lat_t[...], y, preferred_element_type=F32).astype(BF16)
    if sibling:
        total_s, dec_s = refs
        term = nt(x, weights_s[:, at_x]) + nt(y, weights_s[:, at_y])
        total_s[...] = term + total_s_in[...] if carried_s else term
        if stacked:
            for i, ref in enumerate(before):
                dec_s[i] = ref[...]
            dec_s = dec_s.at[stacked]
        dec_s[:n, :] = jnp.dot(lat_s[...], x, preferred_element_type=F32).astype(BF16)
        dec_s[n:, :] = jnp.dot(lat_s[...], y, preferred_element_type=F32).astype(BF16)


def cost(us):
    return pl.CostEstimate(flops=int(us * 1e9), bytes_accessed=1, transcendentals=0)


def kernel_call(body, args, out_shape, us=1):
    return pl.pallas_call(
        body,
        in_specs=[SMEM] + [VMEM] * (len(args) - 1),
        out_specs=jax.tree.map(lambda _: VMEM, out_shape),
        out_shape=out_shape,
        compiler_params=pltpu.CompilerParams(vmem_limit_bytes=VMEM_BYTES),
        cost_estimate=pl.CostEstimate(
            flops=int(us * 1e9),
            bytes_accessed=sum(x.size * x.dtype.itemsize for x in args + jax.tree.leaves(out_shape)),
            transcendentals=0,
        ),
    )(*args)


def step(here, distance, x, y, weights, lat_t, total=None, sibling=None, total_s=None, before=()):
    tokens, width = x.shape
    rows = weights.shape[0]
    grad = jax.ShapeDtypeStruct((tokens, rows), F32)
    block = (2 * rows, width)
    args = [here, x, y, weights, lat_t]
    out_shape = [grad, jax.ShapeDtypeStruct(block, BF16)]
    if sibling:
        args += list(sibling)
        out_shape += [
            grad,
            jax.ShapeDtypeStruct((len(before) + 1,) + block if before else block, BF16),
        ]
    args += [a for a in (total, total_s) if a is not None] + list(before)
    plan = (sibling is not None, total is not None, total_s is not None, len(before))
    return kernel_call(functools.partial(step_kernel, plan, distance), args, out_shape)


def place_kernel(own, here, ex, ey, lat_t, got, *refs):
    blocks, (keep, send) = refs[:own], refs[own:]
    n = lat_t.shape[0]
    half = keep.shape[0]
    nz = 2 * half

    def put(distance, top, bottom):
        chunk = chunk_at(here, distance, nz)
        mine = chunk // half == here[2]

        @pl.when(mine)
        def _():
            keep[chunk % half, :n, :] = top
            keep[chunk % half, n:, :] = bottom

        @pl.when(jnp.logical_not(mine))
        def _():
            send[chunk % half, :n, :] = top
            send[chunk % half, n:, :] = bottom

    put(
        half,
        jnp.dot(lat_t[...], ex[...], preferred_element_type=F32).astype(BF16),
        jnp.dot(lat_t[...], ey[...], preferred_element_type=F32).astype(BF16),
    )
    for k in range(own):
        put(k, blocks[k][:n, :], blocks[k][n:, :])
    for k in range(got.shape[0]):
        put(nz - k - 1, got[k, n:, :], got[k, :n, :])


def place(here, x, y, lat_t, got, blocks):
    part = jax.ShapeDtypeStruct((got.shape[0] + 1,) + blocks[0].shape, BF16)
    body = functools.partial(place_kernel, len(blocks))
    return kernel_call(body, [here, x, y, lat_t, got, *blocks], [part, part], 3)


def join_kernel(here, mine, other, out):
    n = mine.shape[1] // 2
    total = mine[0].astype(F32) + other[0].astype(F32)
    even = here[1] == 0
    out[:, :n] = jnp.where(even, total[:n], total[n:]).astype(BF16)
    out[:, n:] = jnp.where(even, total[n:], total[:n]).astype(BF16)


def join(here, mine, other):
    n, rows, width = other.shape
    return pl.pallas_call(
        join_kernel,
        grid_spec=pltpu.PrefetchScalarGridSpec(
            num_scalar_prefetch=1,
            grid=(n,),
            in_specs=[
                pl.BlockSpec((1, rows, width), lambda i, p: (i, 0, 0)),
                pl.BlockSpec((1, rows, width), lambda i, p: (i, 0, 0)),
            ],
            out_specs=pl.BlockSpec((rows // 2, 2 * width), lambda i, p: (0, i)),
        ),
        out_shape=jax.ShapeDtypeStruct((rows // 2, 2 * n * width), BF16),
        compiler_params=pltpu.CompilerParams(vmem_limit_bytes=VMEM_BYTES),
        cost_estimate=cost(4),
    )(here, mine, other)


def prologue_kernel(block, mask_ref, pre_ref, lat_ref, lat_t_ref):
    first = pl.program_id(0) * (pre_ref.shape[0] // block)
    for i in range(pre_ref.shape[0] // block):
        for j in range(pre_ref.shape[1] // block):
            at = (pl.ds(i * block, block), pl.ds(j * block, block))
            value = jnp.maximum(pre_ref[at].astype(F32), 0.0)
            value = jnp.where(mask_ref[j, first + i] > 0, value, 0.0)
            lat_ref[at] = value.astype(BF16)
            lat_t_ref[at[1], at[0]] = value.T.astype(BF16)


def prologue(block_mask, pre_acts):
    tokens, rows = pre_acts.shape
    block = tokens // block_mask.shape[0]
    n = 4
    return pl.pallas_call(
        functools.partial(prologue_kernel, block),
        grid_spec=pltpu.PrefetchScalarGridSpec(
            num_scalar_prefetch=1,
            grid=(n,),
            in_specs=[pl.BlockSpec((tokens // n, rows), lambda i, p: (i, 0))],
            out_specs=[
                pl.BlockSpec((tokens // n, rows), lambda i, p: (i, 0)),
                pl.BlockSpec((rows, tokens // n), lambda i, p: (0, i)),
            ],
        ),
        out_shape=[
            jax.ShapeDtypeStruct((tokens, rows), BF16),
            jax.ShapeDtypeStruct((rows, tokens), BF16),
        ],
        compiler_params=pltpu.CompilerParams(vmem_limit_bytes=VMEM_BYTES),
        cost_estimate=cost(4),
    )(block_mask.T, pre_acts)


def finish_kernel(here, ex, ey, weights, total, received, live, out):
    nz, width = weights.shape[1] // (2 * ex.shape[1]), ex.shape[1]
    chunk = chunk_at(here, nz // 2, nz)
    term = nt(ex[...], weights[:, column(chunk, here[1], width)])
    term += nt(ey[...], weights[:, column(chunk, 1 - here[1], width)])
    out[...] = jnp.where(live[...] > 0, term + total[...] + received[...], 0.0).astype(BF16)


def finish(here, x, y, weights, total, received, latents):
    out_shape = jax.ShapeDtypeStruct(latents.shape, BF16)
    return kernel_call(finish_kernel, [here, x, y, weights, total, received, latents], out_shape)


def sum_of(got):
    total = got[0].astype(F32)
    for i in range(1, got.shape[0]):
        total += got[i].astype(F32)
    return total.astype(BF16)


def sum_kernel(got, out):
    out[...] = sum_of(got)


def sum_part(got):
    return pl.pallas_call(
        sum_kernel,
        out_shape=jax.ShapeDtypeStruct(got.shape[1:], BF16),
        compiler_params=pltpu.CompilerParams(vmem_limit_bytes=VMEM_BYTES),
        cost_estimate=COST,
    )(got)


def spread_kernel(got, out):
    out[...] = jnp.broadcast_to(sum_of(got)[None], out.shape)


def exchange(terms, axis):
    n = lax.axis_size(axis)
    return lax.all_to_all(terms.reshape(n, terms.shape[0] // n, terms.shape[1]), axis, 0, 0)


def spread(got, axis):
    copies = pl.pallas_call(
        spread_kernel,
        out_shape=jax.ShapeDtypeStruct(got.shape, BF16),
        compiler_params=pltpu.CompilerParams(vmem_limit_bytes=VMEM_BYTES),
        cost_estimate=COST,
    )(got)
    return lax.all_to_all(copies, axis, 0, 0).reshape(-1, got.shape[2])


def input_kernel(delta, encoder, out):
    out[...] = nt(delta[...], encoder[...]).astype(BF16)


def input_part(delta, encoder):
    return pl.pallas_call(
        input_kernel,
        out_shape=jax.ShapeDtypeStruct((delta.shape[0], encoder.shape[0]), BF16),
        compiler_params=pltpu.CompilerParams(vmem_limit_bytes=VMEM_BYTES),
        cost_estimate=COST,
    )(delta, encoder)


def encoder_kernel(here, inputs, delta, keep, send):
    total = lax.dot_general(
        inputs[...], delta[...], (((0,), (0,)), ((), ())), preferred_element_type=F32
    )
    rows = keep.shape[0]
    low = here[2] == 0
    keep[...] = jnp.where(low, total[:rows], total[rows:])
    send[...] = jnp.where(low, total[rows:], total[:rows])


def encoder_part(here, inputs, delta):
    part = jax.ShapeDtypeStruct((inputs.shape[1] // 2, delta.shape[1]), F32)
    return kernel_call(encoder_kernel, [here, inputs, delta], [part, part], us=3)


def shards(errors, decoder, pre_acts, inputs, encoder, block_mask):
    n = lax.axis_size("lat")
    nz = n // 2
    me = lax.axis_index("lat")
    mine = lax.axis_index("tok")
    here = jnp.stack([me // 2, me % 2, mine]).astype(jnp.int32)
    swap = [(i, i ^ 1) for i in range(n)]
    ring = [(2 * k + c, 2 * ((k + 1 - 2 * c) % nz) + c) for k in range(nz) for c in range(2)]
    tok_swap = [(0, 1), (1, 0)]

    across = [(2 * k + c, 2 * ((k + 2 * c - 1) % nz) + 1 - c) for k in range(nz) for c in range(2)]

    own = errors[0]
    weights = decoder[0]
    x = lax.ppermute(own, "lat", ring)
    y = lax.ppermute(own, "lat", across)
    latents, lat_t = prologue(block_mask, pre_acts)
    _, _, lat_t = lax.optimization_barrier((x, y, lat_t))
    sibling = (lax.ppermute(weights, "lat", swap), lax.ppermute(lat_t, "lat", swap))
    last = nz // 2 - 1
    blocks, blocks_s, total, total_s = [], [], None, None
    for k in range(1, last + 1):
        if k == 2:
            x, near, total = lax.optimization_barrier((x, own, total))
            sib = lax.ppermute(near, "lat", swap)
            total, dec = step(here, 0, own, sib, weights, lat_t, total)
            blocks.insert(0, dec)
        elif k > 2:
            x, total = lax.optimization_barrier((x, total))
        nx = lax.ppermute(x, "lat", ring)
        ny = lax.ppermute(y, "lat", ring) if k < last else None
        before = blocks_s if k == last else []
        total, dec, total_s, dec_s = step(
            here, k, x, y, weights, lat_t, total, sibling, total_s, before
        )
        blocks.append(dec)
        blocks_s.append(dec_s)
        x, y = nx, ny
    x, total, total_s, dec_s = lax.optimization_barrier((x, total, total_s, dec_s))
    received = lax.ppermute(total_s, "lat", swap)
    y = lax.ppermute(x, "lat", swap)
    grad_part = finish(here, x, y, weights, total, received, latents)

    grad_part, dec_s = lax.optimization_barrier((grad_part, dec_s))
    dec_got = lax.ppermute(dec_s, "lat", swap)
    terms = exchange(grad_part, "tgt")
    keep, send = place(here, x, y, lat_t, dec_got, blocks)
    terms, send = lax.optimization_barrier((terms, send))
    other = lax.ppermute(send, "tok", tok_swap)
    delta = spread(terms, "tgt")

    terms = exchange(input_part(delta, encoder), "lat")
    enc_keep, enc_send = encoder_part(here, inputs, delta)
    enc_other = lax.ppermute(enc_send, "tok", tok_swap)
    dec_grad = join(here, keep, other)[None]
    enc_grad = enc_keep + enc_other
    terms, dec_grad, enc_grad = lax.optimization_barrier((terms, dec_grad, enc_grad))
    input_grad = lax.all_gather(sum_part(terms), "lat", axis=0, tiled=True)
    return (dec_grad, enc_grad, input_grad)


def solution(mesh):
    in_specs = (
        P("tgt", "tok", "lat"),
        P("tgt", "lat", None),
        P("tok", "lat"),
        P("tok", "tgt"),
        P("tgt", "lat"),
        P("tok", "lat"),
    )
    out_specs = (P("tgt", "lat", "tok"), P(("tgt", "tok"), "lat"), P("tok", "tgt"))
    return jax.shard_map(shards, mesh=mesh, in_specs=in_specs, out_specs=out_specs, check_vma=False)
```

time: 246 us -> 166 us (0.67)
  blocking collectives: 131 us -> 16.8 us
  starting transfers between devices: 0.12 us -> 75.8 us
  waiting for transfers between devices: 76.8 us -> 34.1 us
  Pallas kernels: 0 us -> 23.5 us
  matrix products: 17.4 us -> 0 us
  between operations: 13.8 us -> 0.95 us
  local copies, waits for them, and re-layouts: 2.19 us -> 12.7 us
    psum x2 -> x0, blocking collectives: 131 us -> none  [the longest x1 69.8 us: shards(): input_grad = lax.psum(input_part, 'lat').astype(jnp.bfloat16)]
    all_gather x1 -> x0, waiting for transfers between devices: 76.1 us -> none  [shards(): whole = lax.all_gather(errors[0], 'lat', axis=1, tiled=True)]
    ppermute x0 -> x15, starting transfers between devices: none -> 54.4 us  [the longest x3 10.5 us: shards(): nx = lax.ppermute(x, 'lat', ring)]
    pallas_call x0 -> x12, Pallas kernels: none -> 23.5 us  [the longest x7 16.2 us: kernel_call(): pl.pallas_call(body, in_specs=[SMEM] + [VMEM] * (len(args) - 1), out_spec...]
    all_to_all x0 -> x3, starting transfers between devices: none -> 21.4 us  [the longest x2 14.7 us: exchange(): lax.all_to_all(terms.reshape(n, terms.shape[0] // n, terms.shape[1]), axi...]
    ppermute x0 -> x15, waiting for transfers between devices: none -> 18.5 us  [the longest x1 5.49 us: shards(): other = lax.ppermute(send, 'tok', tok_swap)]
    dot_general x4 -> x0, matrix products: 17.4 us -> none  [the longest x1 7.28 us: dense_products(): lax.dot_general(latents, whole, (((0,), (0,)), ((), ())), preferred_eleme...]
    all_gather x0 -> x1, blocking collectives: none -> 16.8 us  [shards(): input_grad = lax.all_gather(sum_part(terms), 'lat', axis=0, tiled=True)]
  transfers between devices with their start and end apart: 3 -> 18, of which waited for: 1 -> 10; matrix products, arithmetic and copies ran while one was open for 5% -> 0% of each run, Pallas kernels for 0% -> 13%
where the time goes in v2:
time: 166 us; the launch traced here: 165 us
  starting transfers between devices  75.8 us (46%)
  waiting for transfers between devices  34.1 us (21%)
  Pallas kernels  23.5 us (14%)
  blocking collectives  16.8 us (10%)
  local copies, waits for them, and re-layouts  12.7 us (8%)
    all_gather x1, blocking collectives, shards(): input_grad = lax.all_gather(sum_part(terms), 'lat', axis=0, tiled=True)  16.8 us
    pallas_call x7, Pallas kernels, kernel_call(): pl.pallas_call(body, in_specs=[SMEM] + [VMEM] * (len(args) - 1), out_spec...  16.2 us
    all_to_all x2, starting transfers between devices, exchange(): lax.all_to_all(terms.reshape(n, terms.shape[0] // n, terms.shape[1]), axi...  14.7 us
    unnamed x45, local copies, waits for them, and re-layouts  12.7 us
    ppermute x3, starting transfers between devices, shards(): nx = lax.ppermute(x, 'lat', ring)  10.5 us
    all_to_all x1, waiting for transfers between devices, spread(): return lax.all_to_all(copies, axis, 0, 0).reshape(-1, got.shape[2])  9.37 us
    ppermute x1, starting transfers between devices, shards(): lax.ppermute(weights, 'lat', swap)  8.79 us
    all_to_all x1, starting transfers between devices, spread(): return lax.all_to_all(copies, axis, 0, 0).reshape(-1, got.shape[2])  6.71 us
  transfers between devices with their start and end apart: 18, of which 10 were waited for; matrix products, arithmetic and copies ran while one was open for 0% of the time, Pallas kernels for 13%

profile of v2, /device:TPU:1, one launch (start us, length us, event | category | flops | bytes accessed | tf_op | source)
XLA Modules:
  0.0 164.6 jit_solution(17467068976975424483)
XLA Ops:
  0.6 8.8 %collective-permute-start.3 = (bf16[256,4096]{1,0:T(8,128)(2,1)}, bf16[256,4096]{1,0:T(8,128)(2,1)}, u32[]{:S(2)}, u32[]{:S(2)}) collective-permute-start(bf16[256,4096]{1,0:T(8,128)(2,1)} %bitcast.10), channel_id=1, source_target_pairs={{0,32},{32,0},{64,96},{96,64},{128,160},{160,128},{192,224},{224,1... | collective-permute-start | bytes 6291464 | tf_op jit(solution)/shard_map/ppermute | solution.py:294
  11.4 5.3 %collective-permute-start = (bf16[1024,256]{1,0:T(8,128)(2,1)}, bf16[1024,256]{1,0:T(8,128)(2,1)}, u32[]{:S(2)}, u32[]{:S(2)}) collective-permute-start(bf16[1024,256]{1,0:T(8,128)(2,1)} %bitcast.19), channel_id=1, source_target_pairs={{0,64},{32,480},{64,128},{96,32},{128,192},{160,96},{192,256},{224... | collective-permute-start | bytes 1572872 | tf_op jit(solution)/shard_map/ppermute | solution.py:290
  20.3 4.4 %collective-permute-done.2.refs_1_ = bf16[1024,256]{1,0:T(8,128)(2,1)S(1)} collective-permute-done((bf16[1024,256]{1,0:T(8,128)(2,1)}, bf16[1024,256]{1,0:T(8,128)(2,1)S(1)}, u32[]{:S(2)}, u32[]{:S(2)}) %collective-permute-start.2) | collective-permute-done | bytes 524320 | tf_op jit(solution)/shard_map/ppermute | solution.py:291
  24.7 2.6 %collective-permute-done.refs_0_ = bf16[1024,256]{1,0:T(8,128)(2,1)} collective-permute-done((bf16[1024,256]{1,0:T(8,128)(2,1)}, bf16[1024,256]{1,0:T(8,128)(2,1)}, u32[]{:S(2)}, u32[]{:S(2)}) %collective-permute-start) | collective-permute-done | bytes 524320 | tf_op jit(solution)/shard_map/ppermute | solution.py:290
  27.3 2.5 %collective-permute-start.4 = (bf16[256,1024]{1,0:T(8,128)(2,1)S(1)}, bf16[256,1024]{1,0:T(8,128)(2,1)S(1)}, u32[]{:S(2)}, u32[]{:S(2)}) collective-permute-start(bf16[256,1024]{1,0:T(8,128)(2,1)S(1)} %get-tuple-element.41.refs_3_.lat_t), channel_id=1, source_target_pairs={{0,32},{32,0},{64,96},{96,64},{128,160},{160,128},{192,224},{224,1... | collective-permute-start | bytes 1572872 | tf_op jit(solution)/shard_map/ppermute | solution.py:294
  29.8 4.5 %collective-permute-start.1 = (bf16[1024,256]{1,0:T(8,128)(2,1)}, bf16[1024,256]{1,0:T(8,128)(2,1)}, u32[]{:S(2)}, u32[]{:S(2)}) collective-permute-start(bf16[1024,256]{1,0:T(8,128)(2,1)} %collective-permute-done.refs_0_), channel_id=1, source_target_pairs={{0,64},{32,480},{64,128},{96,32},{128,192},{160,96},{192,256},{224... | collective-permute-start | bytes 1572872 | tf_op jit(solution)/shard_map/ppermute | solution.py:305
  37.5 3.0 %shard_map.86 = (f32[1024,256]{1,0:T(8,128)S(1)}, bf16[512,256]{1,0:T(8,128)(2,1)S(1)}, f32[1024,256]{1,0:T(8,128)S(1)}, bf16[512,256]{1,0:T(8,128)(2,1)S(1)}) custom-call(s32[3]{0:T(128)S(1)} %pad_add_fusion.here, bf16[1024,256]{1,0:T(8,128)(2,1)} %collective-permute-done.refs_0_, bf16[1024,256]{1,0:T(8,128)(2,1)S(1)} %copy-done.5, ...), custom_call_target="tpu_custom_call" | custom-call | flops 1000000000 | bytes 8912908 | tf_op jit(solution)/shard_map/pallas_call | solution.py:65
  40.7 3.7 %collective-permute-start.7 = (bf16[1024,256]{1,0:T(8,128)(2,1)S(1)}, bf16[1024,256]{1,0:T(8,128)(2,1)S(1)}, u32[]{:S(2)}, u32[]{:S(2)}) collective-permute-start(bf16[1024,256]{1,0:T(8,128)(2,1)S(1)} %bitcast.20), channel_id=1, source_target_pairs={{0,32},{32,0},{64,96},{96,64},{128,160},{160,128},{192,224},{224,1... | collective-permute-start | bytes 1572872 | tf_op jit(solution)/shard_map/ppermute | solution.py:300
  44.4 3.6 %collective-permute-start.5 = (bf16[1024,256]{1,0:T(8,128)(2,1)}, bf16[1024,256]{1,0:T(8,128)(2,1)S(1)}, u32[]{:S(2)}, u32[]{:S(2)}) collective-permute-start(bf16[1024,256]{1,0:T(8,128)(2,1)} %collective-permute-done.1.refs_0_), channel_id=1, source_target_pairs={{0,64},{32,480},{64,128},{96,32},{128,192},{160,96},{192,256},{224... | collective-permute-start | bytes 1572872 | tf_op jit(solution)/shard_map/ppermute | solution.py:305
  48.1 3.1 %collective-permute-start.9 = (bf16[1024,256]{1,0:T(8,128)(2,1)S(1)}, bf16[1024,256]{1,0:T(8,128)(2,1)S(1)}, u32[]{:S(2)}, u32[]{:S(2)}) collective-permute-start(bf16[1024,256]{1,0:T(8,128)(2,1)S(1)} %collective-permute-done.6.refs_1_), channel_id=1, source_target_pairs={{0,64},{32,480},{64,128},{96,32},{128,192},{160,96},{192,256},{224... | collective-permute-start | bytes 1572872 | tf_op jit(solution)/shard_map/ppermute | solution.py:306
  53.3 3.1 %shard_map.88 = (f32[1024,256]{1,0:T(8,128)S(1)}, bf16[512,256]{1,0:T(8,128)(2,1)S(1)}, f32[1024,256]{1,0:T(8,128)S(1)}, bf16[512,256]{1,0:T(8,128)(2,1)S(1)}) custom-call(s32[3]{0:T(128)S(1)} %pad_add_fusion.here, bf16[1024,256]{1,0:T(8,128)(2,1)} %collective-permute-done.1.refs_0_, bf16[1024,256]{1,0:T(8,128)(2,1)S(1)} %collective-permute-done.6.refs_1_, ...), custom_call_target="tpu_custom_call" | custom-call | flops 1000000000 | bytes 11010060 | tf_op jit(solution)/shard_map/pallas_call | solution.py:65
  60.5 3.8 %shard_map.89 = (f32[1024,256]{1,0:T(8,128)S(1)}, bf16[512,256]{1,0:T(8,128)(2,1)S(1)}, f32[1024,256]{1,0:T(8,128)S(1)}, bf16[3,512,256]{2,1,0:T(8,128)(2,1)}) custom-call(s32[3]{0:T(128)S(1)} %pad_add_fusion.here, bf16[1024,256]{1,0:T(8,128)(2,1)S(1)} %collective-permute-done.5.refs_0_, bf16[1024,256]{1,0:T(8,128)(2,1)S(1)} %collective-permute-done.9.refs_1_, ...), custom_call_target="tpu_custom_call" | custom-call | flops 1000000000 | bytes 12058636 | tf_op jit(solution)/shard_map/pallas_call | solution.py:65
  64.3 2.9 %collective-permute-done.8.ex = bf16[1024,256]{1,0:T(8,128)(2,1)S(1)} collective-permute-done((bf16[1024,256]{1,0:T(8,128)(2,1)S(1)}, bf16[1024,256]{1,0:T(8,128)(2,1)S(1)}, u32[]{:S(2)}, u32[]{:S(2)}) %collective-permute-start.8) | collective-permute-done | bytes 524320 | tf_op jit(solution)/shard_map/ppermute | solution.py:305
  67.2 3.9 %collective-permute-start.11 = (f32[1024,256]{1,0:T(8,128)S(1)}, f32[1024,256]{1,0:T(8,128)S(1)}, u32[]{:S(2)}, u32[]{:S(2)}) collective-permute-start(f32[1024,256]{1,0:T(8,128)S(1)} %get-tuple-element.59), channel_id=1, source_target_pairs={{0,32},{32,0},{64,96},{96,64},{128,160},{160,128},{192,224},{224,1... | collective-permute-start | bytes 3145736 | tf_op jit(solution)/shard_map/ppermute | solution.py:315
  78.8 7.9 %all-to-all-start = ((bf16[16,64,256]{2,1,0:T(8,128)(2,1)}), bf16[16,64,256]{2,1,0:T(8,128)(2,1)S(1)}, u32[]{:S(2)}, u32[]{:S(2)}) async-start(bf16[16,64,256]{2,1,0:T(8,128)(2,1)} %bitcast.6), calls=%async_computation | async-start | bytes 1048576 | tf_op jit(solution)/shard_map/all_to_all | solution.py:235
  95.9 4.4 %all-to-all-done.got = bf16[16,64,256]{2,1,0:T(8,128)(2,1)S(1)} async-done(((bf16[16,64,256]{2,1,0:T(8,128)(2,1)}), bf16[16,64,256]{2,1,0:T(8,128)(2,1)S(1)}, u32[]{:S(2)}, u32[]{:S(2)}) %all-to-all-start) | async-done | bytes 524320 | tf_op jit(solution)/shard_map/all_to_all | solution.py:235
  101.2 6.7 %all-to-all-start.1 = ((bf16[16,64,256]{2,1,0:T(8,128)(2,1)}), bf16[16,64,256]{2,1,0:T(8,128)(2,1)S(1)}, u32[]{:S(2)}, u32[]{:S(2)}) async-start(bf16[16,64,256]{2,1,0:T(8,128)(2,1)} %shard_map.92), calls=%async_computation.1 | async-start | bytes 1048576 | tf_op jit(solution)/shard_map/all_to_all | solution.py:245
  107.9 4.4 %collective-permute-start.13 = (bf16[4,512,256]{2,1,0:T(8,128)(2,1)}, bf16[4,512,256]{2,1,0:T(8,128)(2,1)}, u32[]{:S(2)}, u32[]{:S(2)}) collective-permute-start(bf16[4,512,256]{2,1,0:T(8,128)(2,1)} %get-tuple-element.71), channel_id=1, source_target_pairs={{0,1},{1,0},{2,3},{3,2},{4,5},{5,4},{6,7},{7,6},{8,9},{9,8},{10,11... | collective-permute-start | bytes 3145736 | tf_op jit(solution)/shard_map/ppermute | solution.py:324
  112.3 9.4 %all-to-all-done.1 = bf16[16,64,256]{2,1,0:T(8,128)(2,1)S(1)} async-done(((bf16[16,64,256]{2,1,0:T(8,128)(2,1)}), bf16[16,64,256]{2,1,0:T(8,128)(2,1)S(1)}, u32[]{:S(2)}, u32[]{:S(2)}) %all-to-all-start.1) | async-done | bytes 524320 | tf_op jit(solution)/shard_map/all_to_all | solution.py:245
  122.8 6.8 %all-to-all-start.2 = ((bf16[16,64,256]{2,1,0:T(8,128)(2,1)}), bf16[16,64,256]{2,1,0:T(8,128)(2,1)S(1)}, u32[]{:S(2)}, u32[]{:S(2)}) async-start(bf16[16,64,256]{2,1,0:T(8,128)(2,1)} %bitcast.8), calls=%async_computation.2 | async-start | bytes 1048576 | tf_op jit(solution)/shard_map/all_to_all | solution.py:235
  130.5 4.4 %collective-permute-start.14 = (f32[128,256]{1,0:T(8,128)S(1)}, f32[128,256]{1,0:T(8,128)S(1)}, u32[]{:S(2)}, u32[]{:S(2)}) collective-permute-start(f32[128,256]{1,0:T(8,128)S(1)} %get-tuple-element.73), channel_id=1, source_target_pairs={{0,1},{1,0},{2,3},{3,2},{4,5},{5,4},{6,7},{7,6},{8,9},{9,8},{10,11... | collective-permute-start | bytes 393224 | tf_op jit(solution)/shard_map/ppermute | solution.py:329
  134.9 5.5 %collective-permute-done.13.other = bf16[4,512,256]{2,1,0:T(8,128)(2,1)} collective-permute-done((bf16[4,512,256]{2,1,0:T(8,128)(2,1)}, bf16[4,512,256]{2,1,0:T(8,128)(2,1)}, u32[]{:S(2)}, u32[]{:S(2)}) %collective-permute-start.13) | collective-permute-done | bytes 1048608 | tf_op jit(solution)/shard_map/ppermute | solution.py:324
  140.4 4.0 %shard_map.94 = bf16[256,2048]{1,0:T(8,128)(2,1)} custom-call(s32[3]{0:T(128)S(1)} %pad_add_fusion.here, bf16[4,512,256]{2,1,0:T(8,128)(2,1)S(1)} %copy-done.21, bf16[4,512,256]{2,1,0:T(8,128)(2,1)} %collective-permute-done.13.other), custom_call_target="tpu_custom_call" | custom-call | flops 4000000000 | bytes 1 | tf_op jit(solution)/shard_map/pallas_call | solution.py:144
  147.0 16.8 %all_gather.3 = bf16[1024,256]{1,0:T(8,128)(2,1)S(1)} all-gather(bf16[64,256]{1,0:T(8,128)(2,1)S(1)} %shard_map.96), channel_id=1, replica_groups=mesh['lat'=16,'tgt'=16,'tok'=2] {'lat'}, dimensions={0}, use_global_device_ids=true | all-gather | bytes 557056 | tf_op jit(solution)/shard_map/all_gather | solution.py:333
  (72 shorter events, 38.1 us)
Async XLA Ops:
  0.6 35.8 %collective-permute-start.3 = (bf16[256,4096]{1,0:T(8,128)(2,1)}, bf16[256,4096]{1,0:T(8,128)(2,1)}, u32[]{:S(2)}, u32[]{:S(2)}) collective-permute-start(bf16[256,4096]{1,0:T(8,128)(2,1)} %bitcast.10), channel_id=1, source_target_pairs={{0,32},{32,0},{64,96},{96,64},{128,160},{160,128},{192,224},{224,1... | collective-permute-start | bytes 6291464 | tf_op jit(solution)/shard_map/ppermute | solution.py:294
  9.4 15.3 %collective-permute-start.2 = (bf16[1024,256]{1,0:T(8,128)(2,1)}, bf16[1024,256]{1,0:T(8,128)(2,1)S(1)}, u32[]{:S(2)}, u32[]{:S(2)}) collective-permute-start(bf16[1024,256]{1,0:T(8,128)(2,1)} %bitcast.18), channel_id=1, source_target_pairs={{0,480},{32,64},{64,32},{96,128},{128,96},{160,192},{192,160},{224... | collective-permute-start | bytes 1572872 | tf_op jit(solution)/shard_map/ppermute | solution.py:291
  11.4 16.0 %collective-permute-start = (bf16[1024,256]{1,0:T(8,128)(2,1)}, bf16[1024,256]{1,0:T(8,128)(2,1)}, u32[]{:S(2)}, u32[]{:S(2)}) collective-permute-start(bf16[1024,256]{1,0:T(8,128)(2,1)} %bitcast.19), channel_id=1, source_target_pairs={{0,64},{32,480},{64,128},{96,32},{128,192},{160,96},{192,256},{224... | collective-permute-start | bytes 1572872 | tf_op jit(solution)/shard_map/ppermute | solution.py:290
  18.4 18.1 %copy-start = (bf16[1,256,4096]{2,1,0:T(8,128)(2,1)S(1)}, bf16[1,256,4096]{2,1,0:T(8,128)(2,1)}, u32[]{:S(2)}) copy-start(bf16[1,256,4096]{2,1,0:T(8,128)(2,1)} %param.7) | copy-start | bytes 6291460
  27.3 9.1 %collective-permute-start.4 = (bf16[256,1024]{1,0:T(8,128)(2,1)S(1)}, bf16[256,1024]{1,0:T(8,128)(2,1)S(1)}, u32[]{:S(2)}, u32[]{:S(2)}) collective-permute-start(bf16[256,1024]{1,0:T(8,128)(2,1)S(1)} %get-tuple-element.41.refs_3_.lat_t), channel_id=1, source_target_pairs={{0,32},{32,0},{64,96},{96,64},{128,160},{160,128},{192,224},{224,1... | collective-permute-start | bytes 1572872 | tf_op jit(solution)/shard_map/ppermute | solution.py:294
  29.8 10.9 %collective-permute-start.1 = (bf16[1024,256]{1,0:T(8,128)(2,1)}, bf16[1024,256]{1,0:T(8,128)(2,1)}, u32[]{:S(2)}, u32[]{:S(2)}) collective-permute-start(bf16[1024,256]{1,0:T(8,128)(2,1)} %collective-permute-done.refs_0_), channel_id=1, source_target_pairs={{0,64},{32,480},{64,128},{96,32},{128,192},{160,96},{192,256},{224... | collective-permute-start | bytes 1572872 | tf_op jit(solution)/shard_map/ppermute | solution.py:305
  34.4 13.7 %collective-permute-start.6 = (bf16[1024,256]{1,0:T(8,128)(2,1)}, bf16[1024,256]{1,0:T(8,128)(2,1)S(1)}, u32[]{:S(2)}, u32[]{:S(2)}) collective-permute-start(bf16[1024,256]{1,0:T(8,128)(2,1)} %copy-done.4), channel_id=1, source_target_pairs={{0,64},{32,480},{64,128},{96,32},{128,192},{160,96},{192,256},{224... | collective-permute-start | bytes 1572872 | tf_op jit(solution)/shard_map/ppermute | solution.py:306
  40.7 10.5 %collective-permute-start.7 = (bf16[1024,256]{1,0:T(8,128)(2,1)S(1)}, bf16[1024,256]{1,0:T(8,128)(2,1)S(1)}, u32[]{:S(2)}, u32[]{:S(2)}) collective-permute-start(bf16[1024,256]{1,0:T(8,128)(2,1)S(1)} %bitcast.20), channel_id=1, source_target_pairs={{0,32},{32,0},{64,96},{96,64},{128,160},{160,128},{192,224},{224,1... | collective-permute-start | bytes 1572872 | tf_op jit(solution)/shard_map/ppermute | solution.py:300
  44.4 12.6 %collective-permute-start.5 = (bf16[1024,256]{1,0:T(8,128)(2,1)}, bf16[1024,256]{1,0:T(8,128)(2,1)S(1)}, u32[]{:S(2)}, u32[]{:S(2)}) collective-permute-start(bf16[1024,256]{1,0:T(8,128)(2,1)} %collective-permute-done.1.refs_0_), channel_id=1, source_target_pairs={{0,64},{32,480},{64,128},{96,32},{128,192},{160,96},{192,256},{224... | collective-permute-start | bytes 1572872 | tf_op jit(solution)/shard_map/ppermute | solution.py:305
  48.1 12.4 %collective-permute-start.9 = (bf16[1024,256]{1,0:T(8,128)(2,1)S(1)}, bf16[1024,256]{1,0:T(8,128)(2,1)S(1)}, u32[]{:S(2)}, u32[]{:S(2)}) collective-permute-start(bf16[1024,256]{1,0:T(8,128)(2,1)S(1)} %collective-permute-done.6.refs_1_), channel_id=1, source_target_pairs={{0,64},{32,480},{64,128},{96,32},{128,192},{160,96},{192,256},{224... | collective-permute-start | bytes 1572872 | tf_op jit(solution)/shard_map/ppermute | solution.py:306
  57.0 10.2 %collective-permute-start.8 = (bf16[1024,256]{1,0:T(8,128)(2,1)S(1)}, bf16[1024,256]{1,0:T(8,128)(2,1)S(1)}, u32[]{:S(2)}, u32[]{:S(2)}) collective-permute-start(bf16[1024,256]{1,0:T(8,128)(2,1)S(1)} %collective-permute-done.5.refs_0_), channel_id=1, source_target_pairs={{0,64},{32,480},{64,128},{96,32},{128,192},{160,96},{192,256},{224... | collective-permute-start | bytes 1572872 | tf_op jit(solution)/shard_map/ppermute | solution.py:305
  60.5 14.5 %copy-start.3 = (bf16[1024,256]{1,0:T(8,128)(2,1)S(1)}, bf16[1024,256]{1,0:T(8,128)(2,1)}, u32[]{:S(2)}) copy-start(bf16[1024,256]{1,0:T(8,128)(2,1)} %copy-done.2) | copy-start | bytes 1572868
  64.3 12.5 %copy-start.17 = (bf16[512,256]{1,0:T(8,128)(2,1)}, bf16[512,256]{1,0:T(8,128)(2,1)S(1)}, u32[]{:S(2)}) copy-start(bf16[512,256]{1,0:T(8,128)(2,1)S(1)} %get-tuple-element.67.refs_3_) | copy-start | bytes 786436
  67.2 7.7 %collective-permute-start.11 = (f32[1024,256]{1,0:T(8,128)S(1)}, f32[1024,256]{1,0:T(8,128)S(1)}, u32[]{:S(2)}, u32[]{:S(2)}) collective-permute-start(f32[1024,256]{1,0:T(8,128)S(1)} %get-tuple-element.59), channel_id=1, source_target_pairs={{0,32},{32,0},{64,96},{96,64},{128,160},{160,128},{192,224},{224,1... | collective-permute-start | bytes 3145736 | tf_op jit(solution)/shard_map/ppermute | solution.py:315
  71.1 3.8 %collective-permute-start.10 = (bf16[1024,256]{1,0:T(8,128)(2,1)S(1)}, bf16[1024,256]{1,0:T(8,128)(2,1)S(1)}, u32[]{:S(2)}, u32[]{:S(2)}) collective-permute-start(bf16[1024,256]{1,0:T(8,128)(2,1)S(1)} %collective-permute-done.8.ex), channel_id=1, source_target_pairs={{0,32},{32,0},{64,96},{96,64},{128,160},{160,128},{192,224},{224,1... | collective-permute-start | bytes 1572872 | tf_op jit(solution)/shard_map/ppermute | solution.py:316
  76.8 9.9 %collective-permute-start.12 = (bf16[3,512,256]{2,1,0:T(8,128)(2,1)}, bf16[3,512,256]{2,1,0:T(8,128)(2,1)S(1)}, u32[]{:S(2)}, u32[]{:S(2)}) collective-permute-start(bf16[3,512,256]{2,1,0:T(8,128)(2,1)} %get-tuple-element.63), channel_id=1, source_target_pairs={{0,32},{32,0},{64,96},{96,64},{128,160},{160,128},{192,224},{224,1... | collective-permute-start | bytes 2359304 | tf_op jit(solution)/shard_map/ppermute | solution.py:320
  78.8 21.5 %all-to-all-start = ((bf16[16,64,256]{2,1,0:T(8,128)(2,1)}), bf16[16,64,256]{2,1,0:T(8,128)(2,1)S(1)}, u32[]{:S(2)}, u32[]{:S(2)}) async-start(bf16[16,64,256]{2,1,0:T(8,128)(2,1)} %bitcast.6), calls=%async_computation | async-start | bytes 1048576 | tf_op jit(solution)/shard_map/all_to_all | solution.py:235
  95.9 25.8 %copy-start.8 = (bf16[256,256]{1,0:T(8,128)(2,1)S(1)}, bf16[256,256]{1,0:T(8,128)(2,1)}, u32[]{:S(2)}) copy-start(bf16[256,256]{1,0:T(8,128)(2,1)} %encoder.1) | copy-start | bytes 393220
  100.3 29.3 %copy-start.12 = (bf16[1024,256]{1,0:T(8,128)(2,1)S(1)}, bf16[1024,256]{1,0:T(8,128)(2,1)}, u32[]{:S(2)}) copy-start(bf16[1024,256]{1,0:T(8,128)(2,1)} %inputs.1) | copy-start | bytes 1572868
  101.2 20.4 %all-to-all-start.1 = ((bf16[16,64,256]{2,1,0:T(8,128)(2,1)}), bf16[16,64,256]{2,1,0:T(8,128)(2,1)S(1)}, u32[]{:S(2)}, u32[]{:S(2)}) async-start(bf16[16,64,256]{2,1,0:T(8,128)(2,1)} %shard_map.92), calls=%async_computation.1 | async-start | bytes 1048576 | tf_op jit(solution)/shard_map/all_to_all | solution.py:245
  107.9 32.4 %collective-permute-start.13 = (bf16[4,512,256]{2,1,0:T(8,128)(2,1)}, bf16[4,512,256]{2,1,0:T(8,128)(2,1)}, u32[]{:S(2)}, u32[]{:S(2)}) collective-permute-start(bf16[4,512,256]{2,1,0:T(8,128)(2,1)} %get-tuple-element.71), channel_id=1, source_target_pairs={{0,1},{1,0},{2,3},{3,2},{4,5},{5,4},{6,7},{7,6},{8,9},{9,8},{10,11... | collective-permute-start | bytes 3145736 | tf_op jit(solution)/shard_map/ppermute | solution.py:324
  122.8 24.1 %all-to-all-start.2 = ((bf16[16,64,256]{2,1,0:T(8,128)(2,1)}), bf16[16,64,256]{2,1,0:T(8,128)(2,1)S(1)}, u32[]{:S(2)}, u32[]{:S(2)}) async-start(bf16[16,64,256]{2,1,0:T(8,128)(2,1)} %bitcast.8), calls=%async_computation.2 | async-start | bytes 1048576 | tf_op jit(solution)/shard_map/all_to_all | solution.py:235
  129.6 10.8 %copy-start.21 = (bf16[4,512,256]{2,1,0:T(8,128)(2,1)S(1)}, bf16[4,512,256]{2,1,0:T(8,128)(2,1)}, u32[]{:S(2)}) copy-start(bf16[4,512,256]{2,1,0:T(8,128)(2,1)} %copy-done.20) | copy-start | bytes 3145732
  130.5 13.9 %collective-permute-start.14 = (f32[128,256]{1,0:T(8,128)S(1)}, f32[128,256]{1,0:T(8,128)S(1)}, u32[]{:S(2)}, u32[]{:S(2)}) collective-permute-start(f32[128,256]{1,0:T(8,128)S(1)} %get-tuple-element.73), channel_id=1, source_target_pairs={{0,1},{1,0},{2,3},{3,2},{4,5},{5,4},{6,7},{7,6},{8,9},{9,8},{10,11... | collective-permute-start | bytes 393224 | tf_op jit(solution)/shard_map/ppermute | solution.py:329
  (16 other events, 30.4 us)

commit v3 on v2

--- a/solution.py
+++ b/solution.py
@@ -287,23 +287,24 @@
 
     own = errors[0]
     weights = decoder[0]
+    latents, lat_t = prologue(block_mask, pre_acts)
+    sibling = (lax.ppermute(weights, "lat", swap), lax.ppermute(lat_t, "lat", swap))
+    y = lax.ppermute(own, "lat", across)
     x = lax.ppermute(own, "lat", ring)
-    y = lax.ppermute(own, "lat", across)
-    latents, lat_t = prologue(block_mask, pre_acts)
-    _, _, lat_t = lax.optimization_barrier((x, y, lat_t))
-    sibling = (lax.ppermute(weights, "lat", swap), lax.ppermute(lat_t, "lat", swap))
+    x, sibling = lax.optimization_barrier((x, sibling))
     last = nz // 2 - 1
     blocks, blocks_s, total, total_s = [], [], None, None
     for k in range(1, last + 1):
         if k == 2:
             x, near, total = lax.optimization_barrier((x, own, total))
             sib = lax.ppermute(near, "lat", swap)
-            total, dec = step(here, 0, own, sib, weights, lat_t, total)
-            blocks.insert(0, dec)
         elif k > 2:
             x, total = lax.optimization_barrier((x, total))
         nx = lax.ppermute(x, "lat", ring)
         ny = lax.ppermute(y, "lat", ring) if k < last else None
+        if k == last:
+            total, dec = step(here, 0, own, sib, weights, lat_t, total)
+            blocks.insert(0, dec)
         before = blocks_s if k == last else []
         total, dec, total_s, dec_s = step(
             here, k, x, y, weights, lat_t, total, sibling, total_s, before

time: 166 us -> 162 us (0.976)
  Pallas kernels: 23.5 us -> 20.6 us
    pallas_call x7, Pallas kernels: 16.2 us -> 13.4 us  [kernel_call(): pl.pallas_call(body, in_specs=[SMEM] + [VMEM] * (len(args) - 1), out_spec...]
    ppermute x1, waiting for transfers between devices: 2.59 us -> 0.01 us  [shards(): x = lax.ppermute(own, 'lat', ring)]
    ppermute x1, starting transfers between devices: 3.72 us -> 1.92 us  [shards(): sib = lax.ppermute(near, 'lat', swap)]
  transfers between devices with their start and end apart: 18 -> 18, of which waited for: 10 -> 8; matrix products, arithmetic and copies ran while one was open for 0% -> 0% of each run, Pallas kernels for 13% -> 11%
where the time goes in v3:
time: 162 us; the launch traced here: 161 us
  starting transfers between devices  75.3 us (46%)
  waiting for transfers between devices  32.8 us (20%)
  Pallas kernels  20.6 us (13%)
  blocking collectives  17.4 us (11%)
  local copies, waits for them, and re-layouts  12.8 us (8%)
    all_gather x1, blocking collectives, shards(): input_grad = lax.all_gather(sum_part(terms), 'lat', axis=0, tiled=True)  17.4 us
    all_to_all x2, starting transfers between devices, exchange(): lax.all_to_all(terms.reshape(n, terms.shape[0] // n, terms.shape[1]), axi...  14 us
    pallas_call x7, Pallas kernels, kernel_call(): pl.pallas_call(body, in_specs=[SMEM] + [VMEM] * (len(args) - 1), out_spec...  13.4 us
    unnamed x45, local copies, waits for them, and re-layouts  12.8 us
    ppermute x3, starting transfers between devices, shards(): nx = lax.ppermute(x, 'lat', ring)  11 us
    all_to_all x1, waiting for transfers between devices, spread(): return lax.all_to_all(copies, axis, 0, 0).reshape(-1, got.shape[2])  9.36 us
    ppermute x1, starting transfers between devices, shards(): lax.ppermute(weights, 'lat', swap)  8.79 us
    all_to_all x2, waiting for transfers between devices, exchange(): lax.all_to_all(terms.reshape(n, terms.shape[0] // n, terms.shape[1]), axi...  7.45 us
  transfers between devices with their start and end apart: 18, of which 8 were waited for; matrix products, arithmetic and copies ran while one was open for 0% of the time, Pallas kernels for 11%

profile of v3, /device:TPU:1, one launch (start us, length us, event | category | flops | bytes accessed | tf_op | source)
XLA Modules:
  0.0 160.6 jit_solution(13692304438748319366)
XLA Ops:
  0.6 8.8 %collective-permute-start.1 = (bf16[256,4096]{1,0:T(8,128)(2,1)}, bf16[256,4096]{1,0:T(8,128)(2,1)S(1)}, u32[]{:S(2)}, u32[]{:S(2)}) collective-permute-start(bf16[256,4096]{1,0:T(8,128)(2,1)} %bitcast.10), channel_id=1, source_target_pairs={{0,32},{32,0},{64,96},{96,64},{128,160},{160,128},{192,224},{224,1... | collective-permute-start | bytes 6291464 | tf_op jit(solution)/shard_map/ppermute | solution.py:291
  9.4 5.3 %collective-permute-start = (bf16[1024,256]{1,0:T(8,128)(2,1)}, bf16[1024,256]{1,0:T(8,128)(2,1)}, u32[]{:S(2)}, u32[]{:S(2)}) collective-permute-start(bf16[1024,256]{1,0:T(8,128)(2,1)} %bitcast.3.refs_0_), channel_id=1, source_target_pairs={{0,64},{32,480},{64,128},{96,32},{128,192},{160,96},{192,256},{224... | collective-permute-start | bytes 1572872 | tf_op jit(solution)/shard_map/ppermute | solution.py:293
  20.3 1.9 %collective-permute-start.4 = (bf16[1024,256]{1,0:T(8,128)(2,1)}, bf16[1024,256]{1,0:T(8,128)(2,1)}, u32[]{:S(2)}, u32[]{:S(2)}) collective-permute-start(bf16[1024,256]{1,0:T(8,128)(2,1)} %bitcast.3.refs_0_), channel_id=1, source_target_pairs={{0,480},{32,64},{64,32},{96,128},{128,96},{160,192},{192,160},{224... | collective-permute-start | bytes 1572872 | tf_op jit(solution)/shard_map/ppermute | solution.py:292
  23.6 4.9 %collective-permute-start.3 = (bf16[1024,256]{1,0:T(8,128)(2,1)}, bf16[1024,256]{1,0:T(8,128)(2,1)}, u32[]{:S(2)}, u32[]{:S(2)}) collective-permute-start(bf16[1024,256]{1,0:T(8,128)(2,1)} %collective-permute-done.refs_0_), channel_id=1, source_target_pairs={{0,64},{32,480},{64,128},{96,32},{128,192},{160,96},{192,256},{224... | collective-permute-start | bytes 1572872 | tf_op jit(solution)/shard_map/ppermute | solution.py:303
  28.6 5.6 %collective-permute-done.4.refs_1_ = bf16[1024,256]{1,0:T(8,128)(2,1)} collective-permute-done((bf16[1024,256]{1,0:T(8,128)(2,1)}, bf16[1024,256]{1,0:T(8,128)(2,1)}, u32[]{:S(2)}, u32[]{:S(2)}) %collective-permute-start.4) | collective-permute-done | bytes 524320 | tf_op jit(solution)/shard_map/ppermute | solution.py:292
  37.8 2.5 %shard_map.86 = (f32[1024,256]{1,0:T(8,128)S(1)}, bf16[512,256]{1,0:T(8,128)(2,1)S(1)}, f32[1024,256]{1,0:T(8,128)S(1)}, bf16[512,256]{1,0:T(8,128)(2,1)S(1)}) custom-call(s32[3]{0:T(128)S(1)} %pad_add_fusion.here, bf16[1024,256]{1,0:T(8,128)(2,1)} %collective-permute-done.refs_0_, bf16[1024,256]{1,0:T(8,128)(2,1)} %collective-permute-done.4.refs_1_, ...), custom_call_target="tpu_custom_call" | custom-call | flops 1000000000 | bytes 8912908 | tf_op jit(solution)/shard_map/pallas_call | solution.py:65
  40.3 2.3 %collective-permute-start.5 = (bf16[1024,256]{1,0:T(8,128)(2,1)}, bf16[1024,256]{1,0:T(8,128)(2,1)S(1)}, u32[]{:S(2)}, u32[]{:S(2)}) collective-permute-start(bf16[1024,256]{1,0:T(8,128)(2,1)} %collective-permute-done.3.refs_0_), channel_id=1, source_target_pairs={{0,64},{32,480},{64,128},{96,32},{128,192},{160,96},{192,256},{224... | collective-permute-start | bytes 1572872 | tf_op jit(solution)/shard_map/ppermute | solution.py:303
  44.7 4.4 %collective-permute-start.8 = (bf16[1024,256]{1,0:T(8,128)(2,1)S(1)}, bf16[1024,256]{1,0:T(8,128)(2,1)S(1)}, u32[]{:S(2)}, u32[]{:S(2)}) collective-permute-start(bf16[1024,256]{1,0:T(8,128)(2,1)S(1)} %collective-permute-done.6.refs_1_), channel_id=1, source_target_pairs={{0,64},{32,480},{64,128},{96,32},{128,192},{160,96},{192,256},{224... | collective-permute-start | bytes 1572872 | tf_op jit(solution)/shard_map/ppermute | solution.py:304
  49.1 2.4 %shard_map.87 = (f32[1024,256]{1,0:T(8,128)S(1)}, bf16[512,256]{1,0:T(8,128)(2,1)S(1)}, f32[1024,256]{1,0:T(8,128)S(1)}, bf16[512,256]{1,0:T(8,128)(2,1)S(1)}) custom-call(s32[3]{0:T(128)S(1)} %pad_add_fusion.here, bf16[1024,256]{1,0:T(8,128)(2,1)} %collective-permute-done.3.refs_0_, bf16[1024,256]{1,0:T(8,128)(2,1)S(1)} %collective-permute-done.6.refs_1_, ...), custom_call_target="tpu_custom_call" | custom-call | flops 1000000000 | bytes 11010060 | tf_op jit(solution)/shard_map/pallas_call | solution.py:65
  52.1 3.8 %collective-permute-start.7 = (bf16[1024,256]{1,0:T(8,128)(2,1)S(1)}, bf16[1024,256]{1,0:T(8,128)(2,1)S(1)}, u32[]{:S(2)}, u32[]{:S(2)}) collective-permute-start(bf16[1024,256]{1,0:T(8,128)(2,1)S(1)} %collective-permute-done.5.refs_0_), channel_id=1, source_target_pairs={{0,64},{32,480},{64,128},{96,32},{128,192},{160,96},{192,256},{224... | collective-permute-start | bytes 1572872 | tf_op jit(solution)/shard_map/ppermute | solution.py:303
  57.8 2.7 %shard_map.89 = (f32[1024,256]{1,0:T(8,128)S(1)}, bf16[512,256]{1,0:T(8,128)(2,1)S(1)}, f32[1024,256]{1,0:T(8,128)S(1)}, bf16[3,512,256]{2,1,0:T(8,128)(2,1)}) custom-call(s32[3]{0:T(128)S(1)} %pad_add_fusion.here, bf16[1024,256]{1,0:T(8,128)(2,1)S(1)} %collective-permute-done.5.refs_0_, bf16[1024,256]{1,0:T(8,128)(2,1)S(1)} %collective-permute-done.8.refs_1_, ...), custom_call_target="tpu_custom_call" | custom-call | flops 1000000000 | bytes 12058636 | tf_op jit(solution)/shard_map/pallas_call | solution.py:65
  60.5 2.0 %collective-permute-done.7.ex = bf16[1024,256]{1,0:T(8,128)(2,1)S(1)} collective-permute-done((bf16[1024,256]{1,0:T(8,128)(2,1)S(1)}, bf16[1024,256]{1,0:T(8,128)(2,1)S(1)}, u32[]{:S(2)}, u32[]{:S(2)}) %collective-permute-start.7) | collective-permute-done | bytes 524320 | tf_op jit(solution)/shard_map/ppermute | solution.py:303
  62.5 4.7 %collective-permute-start.11 = (f32[1024,256]{1,0:T(8,128)S(1)}, f32[1024,256]{1,0:T(8,128)S(1)}, u32[]{:S(2)}, u32[]{:S(2)}) collective-permute-start(f32[1024,256]{1,0:T(8,128)S(1)} %get-tuple-element.63), channel_id=1, source_target_pairs={{0,32},{32,0},{64,96},{96,64},{128,160},{160,128},{192,224},{224,1... | collective-permute-start | bytes 3145736 | tf_op jit(solution)/shard_map/ppermute | solution.py:316
  72.9 2.0 %collective-permute-start.12 = (bf16[3,512,256]{2,1,0:T(8,128)(2,1)}, bf16[3,512,256]{2,1,0:T(8,128)(2,1)S(1)}, u32[]{:S(2)}, u32[]{:S(2)}) collective-permute-start(bf16[3,512,256]{2,1,0:T(8,128)(2,1)} %get-tuple-element.67), channel_id=1, source_target_pairs={{0,32},{32,0},{64,96},{96,64},{128,160},{160,128},{192,224},{224,1... | collective-permute-start | bytes 2359304 | tf_op jit(solution)/shard_map/ppermute | solution.py:321
  74.9 7.9 %all-to-all-start = ((bf16[16,64,256]{2,1,0:T(8,128)(2,1)}), bf16[16,64,256]{2,1,0:T(8,128)(2,1)S(1)}, u32[]{:S(2)}, u32[]{:S(2)}) async-start(bf16[16,64,256]{2,1,0:T(8,128)(2,1)} %bitcast.6), calls=%async_computation | async-start | bytes 1048576 | tf_op jit(solution)/shard_map/all_to_all | solution.py:235
  89.9 6.4 %all-to-all-done.got = bf16[16,64,256]{2,1,0:T(8,128)(2,1)S(1)} async-done(((bf16[16,64,256]{2,1,0:T(8,128)(2,1)}), bf16[16,64,256]{2,1,0:T(8,128)(2,1)S(1)}, u32[]{:S(2)}, u32[]{:S(2)}) %all-to-all-start) | async-done | bytes 524320 | tf_op jit(solution)/shard_map/all_to_all | solution.py:235
  97.3 6.7 %all-to-all-start.1 = ((bf16[16,64,256]{2,1,0:T(8,128)(2,1)}), bf16[16,64,256]{2,1,0:T(8,128)(2,1)S(1)}, u32[]{:S(2)}, u32[]{:S(2)}) async-start(bf16[16,64,256]{2,1,0:T(8,128)(2,1)} %shard_map.92), calls=%async_computation.1 | async-start | bytes 1048576 | tf_op jit(solution)/shard_map/all_to_all | solution.py:245
  104.0 4.4 %collective-permute-start.13 = (bf16[4,512,256]{2,1,0:T(8,128)(2,1)S(1)}, bf16[4,512,256]{2,1,0:T(8,128)(2,1)}, u32[]{:S(2)}, u32[]{:S(2)}) collective-permute-start(bf16[4,512,256]{2,1,0:T(8,128)(2,1)S(1)} %copy-done.10), channel_id=1, source_target_pairs={{0,1},{1,0},{2,3},{3,2},{4,5},{5,4},{6,7},{7,6},{8,9},{9,8},{10,11... | collective-permute-start | bytes 3145736 | tf_op jit(solution)/shard_map/ppermute | solution.py:325
  108.4 9.4 %all-to-all-done.1 = bf16[16,64,256]{2,1,0:T(8,128)(2,1)S(1)} async-done(((bf16[16,64,256]{2,1,0:T(8,128)(2,1)}), bf16[16,64,256]{2,1,0:T(8,128)(2,1)S(1)}, u32[]{:S(2)}, u32[]{:S(2)}) %all-to-all-start.1) | async-done | bytes 524320 | tf_op jit(solution)/shard_map/all_to_all | solution.py:245
  118.8 6.2 %all-to-all-start.2 = ((bf16[16,64,256]{2,1,0:T(8,128)(2,1)}), bf16[16,64,256]{2,1,0:T(8,128)(2,1)S(1)}, u32[]{:S(2)}, u32[]{:S(2)}) async-start(bf16[16,64,256]{2,1,0:T(8,128)(2,1)} %bitcast.8), calls=%async_computation.2 | async-start | bytes 1048576 | tf_op jit(solution)/shard_map/all_to_all | solution.py:235
  125.9 4.4 %collective-permute-start.14 = (f32[128,256]{1,0:T(8,128)S(1)}, f32[128,256]{1,0:T(8,128)S(1)}, u32[]{:S(2)}, u32[]{:S(2)}) collective-permute-start(f32[128,256]{1,0:T(8,128)S(1)} %get-tuple-element.77), channel_id=1, source_target_pairs={{0,1},{1,0},{2,3},{3,2},{4,5},{5,4},{6,7},{7,6},{8,9},{9,8},{10,11... | collective-permute-start | bytes 393224 | tf_op jit(solution)/shard_map/ppermute | solution.py:330
  130.3 6.3 %collective-permute-done.13.other = bf16[4,512,256]{2,1,0:T(8,128)(2,1)} collective-permute-done((bf16[4,512,256]{2,1,0:T(8,128)(2,1)S(1)}, bf16[4,512,256]{2,1,0:T(8,128)(2,1)}, u32[]{:S(2)}, u32[]{:S(2)}) %collective-permute-start.13) | collective-permute-done | bytes 1048608 | tf_op jit(solution)/shard_map/ppermute | solution.py:325
  136.6 4.0 %shard_map.94 = bf16[256,2048]{1,0:T(8,128)(2,1)} custom-call(s32[3]{0:T(128)S(1)} %pad_add_fusion.here, bf16[4,512,256]{2,1,0:T(8,128)(2,1)S(1)} %copy-done.21, bf16[4,512,256]{2,1,0:T(8,128)(2,1)} %collective-permute-done.13.other), custom_call_target="tpu_custom_call" | custom-call | flops 4000000000 | bytes 1 | tf_op jit(solution)/shard_map/pallas_call | solution.py:144
  142.4 17.4 %all_gather.3 = bf16[1024,256]{1,0:T(8,128)(2,1)S(1)} all-gather(bf16[64,256]{1,0:T(8,128)(2,1)S(1)} %shard_map.96), channel_id=1, replica_groups=mesh['lat'=16,'tgt'=16,'tok'=2] {'lat'}, dimensions={0}, use_global_device_ids=true | all-gather | bytes 557056 | tf_op jit(solution)/shard_map/all_gather | solution.py:334
  (72 shorter events, 33.3 us)
Async XLA Ops:
  0.6 21.6 %collective-permute-start.1 = (bf16[256,4096]{1,0:T(8,128)(2,1)}, bf16[256,4096]{1,0:T(8,128)(2,1)S(1)}, u32[]{:S(2)}, u32[]{:S(2)}) collective-permute-start(bf16[256,4096]{1,0:T(8,128)(2,1)} %bitcast.10), channel_id=1, source_target_pairs={{0,32},{32,0},{64,96},{96,64},{128,160},{160,128},{192,224},{224,1... | collective-permute-start | bytes 6291464 | tf_op jit(solution)/shard_map/ppermute | solution.py:291
  9.4 12.8 %collective-permute-start = (bf16[1024,256]{1,0:T(8,128)(2,1)}, bf16[1024,256]{1,0:T(8,128)(2,1)}, u32[]{:S(2)}, u32[]{:S(2)}) collective-permute-start(bf16[1024,256]{1,0:T(8,128)(2,1)} %bitcast.3.refs_0_), channel_id=1, source_target_pairs={{0,64},{32,480},{64,128},{96,32},{128,192},{160,96},{192,256},{224... | collective-permute-start | bytes 1572872 | tf_op jit(solution)/shard_map/ppermute | solution.py:293
  16.5 19.7 %copy-start = (bf16[1,256,4096]{2,1,0:T(8,128)(2,1)S(1)}, bf16[1,256,4096]{2,1,0:T(8,128)(2,1)}, u32[]{:S(2)}) copy-start(bf16[1,256,4096]{2,1,0:T(8,128)(2,1)} %param.7) | copy-start | bytes 6291460
  18.4 3.9 %collective-permute-start.2 = (bf16[256,1024]{1,0:T(8,128)(2,1)S(1)}, bf16[256,1024]{1,0:T(8,128)(2,1)S(1)}, u32[]{:S(2)}, u32[]{:S(2)}) collective-permute-start(bf16[256,1024]{1,0:T(8,128)(2,1)S(1)} %get-tuple-element.42.refs_3_.lat_t), channel_id=1, source_target_pairs={{0,32},{32,0},{64,96},{96,64},{128,160},{160,128},{192,224},{224,1... | collective-permute-start | bytes 1572872 | tf_op jit(solution)/shard_map/ppermute | solution.py:291
  20.3 14.0 %collective-permute-start.4 = (bf16[1024,256]{1,0:T(8,128)(2,1)}, bf16[1024,256]{1,0:T(8,128)(2,1)}, u32[]{:S(2)}, u32[]{:S(2)}) collective-permute-start(bf16[1024,256]{1,0:T(8,128)(2,1)} %bitcast.3.refs_0_), channel_id=1, source_target_pairs={{0,480},{32,64},{64,32},{96,128},{128,96},{160,192},{192,160},{224... | collective-permute-start | bytes 1572872 | tf_op jit(solution)/shard_map/ppermute | solution.py:292
  23.6 16.7 %collective-permute-start.3 = (bf16[1024,256]{1,0:T(8,128)(2,1)}, bf16[1024,256]{1,0:T(8,128)(2,1)}, u32[]{:S(2)}, u32[]{:S(2)}) collective-permute-start(bf16[1024,256]{1,0:T(8,128)(2,1)} %collective-permute-done.refs_0_), channel_id=1, source_target_pairs={{0,64},{32,480},{64,128},{96,32},{128,192},{160,96},{192,256},{224... | collective-permute-start | bytes 1572872 | tf_op jit(solution)/shard_map/ppermute | solution.py:303
  34.2 10.4 %collective-permute-start.6 = (bf16[1024,256]{1,0:T(8,128)(2,1)}, bf16[1024,256]{1,0:T(8,128)(2,1)S(1)}, u32[]{:S(2)}, u32[]{:S(2)}) collective-permute-start(bf16[1024,256]{1,0:T(8,128)(2,1)} %collective-permute-done.4.refs_1_), channel_id=1, source_target_pairs={{0,64},{32,480},{64,128},{96,32},{128,192},{160,96},{192,256},{224... | collective-permute-start | bytes 1572872 | tf_op jit(solution)/shard_map/ppermute | solution.py:304
  40.3 11.9 %collective-permute-start.5 = (bf16[1024,256]{1,0:T(8,128)(2,1)}, bf16[1024,256]{1,0:T(8,128)(2,1)S(1)}, u32[]{:S(2)}, u32[]{:S(2)}) collective-permute-start(bf16[1024,256]{1,0:T(8,128)(2,1)} %collective-permute-done.3.refs_0_), channel_id=1, source_target_pairs={{0,64},{32,480},{64,128},{96,32},{128,192},{160,96},{192,256},{224... | collective-permute-start | bytes 1572872 | tf_op jit(solution)/shard_map/ppermute | solution.py:303
  42.6 13.3 %collective-permute-start.9 = (bf16[1024,256]{1,0:T(8,128)(2,1)}, bf16[1024,256]{1,0:T(8,128)(2,1)S(1)}, u32[]{:S(2)}, u32[]{:S(2)}) collective-permute-start(bf16[1024,256]{1,0:T(8,128)(2,1)} %bitcast.3.refs_0_), channel_id=1, source_target_pairs={{0,32},{32,0},{64,96},{96,64},{128,160},{160,128},{192,224},{224,1... | collective-permute-start | bytes 1572872 | tf_op jit(solution)/shard_map/ppermute | solution.py:300
  44.7 13.1 %collective-permute-start.8 = (bf16[1024,256]{1,0:T(8,128)(2,1)S(1)}, bf16[1024,256]{1,0:T(8,128)(2,1)S(1)}, u32[]{:S(2)}, u32[]{:S(2)}) collective-permute-start(bf16[1024,256]{1,0:T(8,128)(2,1)S(1)} %collective-permute-done.6.refs_1_), channel_id=1, source_target_pairs={{0,64},{32,480},{64,128},{96,32},{128,192},{160,96},{192,256},{224... | collective-permute-start | bytes 1572872 | tf_op jit(solution)/shard_map/ppermute | solution.py:304
  52.1 10.3 %collective-permute-start.7 = (bf16[1024,256]{1,0:T(8,128)(2,1)S(1)}, bf16[1024,256]{1,0:T(8,128)(2,1)S(1)}, u32[]{:S(2)}, u32[]{:S(2)}) collective-permute-start(bf16[1024,256]{1,0:T(8,128)(2,1)S(1)} %collective-permute-done.5.refs_0_), channel_id=1, source_target_pairs={{0,64},{32,480},{64,128},{96,32},{128,192},{160,96},{192,256},{224... | collective-permute-start | bytes 1572872 | tf_op jit(solution)/shard_map/ppermute | solution.py:303
  57.8 13.2 %copy-start.5 = (bf16[1024,256]{1,0:T(8,128)(2,1)S(1)}, bf16[1024,256]{1,0:T(8,128)(2,1)}, u32[]{:S(2)}) copy-start(bf16[1024,256]{1,0:T(8,128)(2,1)} %copy-done.4) | copy-start | bytes 1572868
  60.5 12.4 %copy-start.17 = (bf16[512,256]{1,0:T(8,128)(2,1)}, bf16[512,256]{1,0:T(8,128)(2,1)S(1)}, u32[]{:S(2)}) copy-start(bf16[512,256]{1,0:T(8,128)(2,1)S(1)} %get-tuple-element.71.refs_3_) | copy-start | bytes 786436
  62.5 8.5 %collective-permute-start.11 = (f32[1024,256]{1,0:T(8,128)S(1)}, f32[1024,256]{1,0:T(8,128)S(1)}, u32[]{:S(2)}, u32[]{:S(2)}) collective-permute-start(f32[1024,256]{1,0:T(8,128)S(1)} %get-tuple-element.63), channel_id=1, source_target_pairs={{0,32},{32,0},{64,96},{96,64},{128,160},{160,128},{192,224},{224,1... | collective-permute-start | bytes 3145736 | tf_op jit(solution)/shard_map/ppermute | solution.py:316
  67.2 3.8 %collective-permute-start.10 = (bf16[1024,256]{1,0:T(8,128)(2,1)S(1)}, bf16[1024,256]{1,0:T(8,128)(2,1)S(1)}, u32[]{:S(2)}, u32[]{:S(2)}) collective-permute-start(bf16[1024,256]{1,0:T(8,128)(2,1)S(1)} %collective-permute-done.7.ex), channel_id=1, source_target_pairs={{0,32},{32,0},{64,96},{96,64},{128,160},{160,128},{192,224},{224,1... | collective-permute-start | bytes 1572872 | tf_op jit(solution)/shard_map/ppermute | solution.py:317
  72.9 9.9 %collective-permute-start.12 = (bf16[3,512,256]{2,1,0:T(8,128)(2,1)}, bf16[3,512,256]{2,1,0:T(8,128)(2,1)S(1)}, u32[]{:S(2)}, u32[]{:S(2)}) collective-permute-start(bf16[3,512,256]{2,1,0:T(8,128)(2,1)} %get-tuple-element.67), channel_id=1, source_target_pairs={{0,32},{32,0},{64,96},{96,64},{128,160},{160,128},{192,224},{224,1... | collective-permute-start | bytes 2359304 | tf_op jit(solution)/shard_map/ppermute | solution.py:321
  74.9 21.5 %all-to-all-start = ((bf16[16,64,256]{2,1,0:T(8,128)(2,1)}), bf16[16,64,256]{2,1,0:T(8,128)(2,1)S(1)}, u32[]{:S(2)}, u32[]{:S(2)}) async-start(bf16[16,64,256]{2,1,0:T(8,128)(2,1)} %bitcast.6), calls=%async_computation | async-start | bytes 1048576 | tf_op jit(solution)/shard_map/all_to_all | solution.py:235
  89.9 27.8 %copy-start.8 = (bf16[256,256]{1,0:T(8,128)(2,1)S(1)}, bf16[256,256]{1,0:T(8,128)(2,1)}, u32[]{:S(2)}) copy-start(bf16[256,256]{1,0:T(8,128)(2,1)} %encoder.1) | copy-start | bytes 393220
  96.4 28.6 %copy-start.12 = (bf16[1024,256]{1,0:T(8,128)(2,1)S(1)}, bf16[1024,256]{1,0:T(8,128)(2,1)}, u32[]{:S(2)}) copy-start(bf16[1024,256]{1,0:T(8,128)(2,1)} %inputs.1) | copy-start | bytes 1572868
  97.3 20.4 %all-to-all-start.1 = ((bf16[16,64,256]{2,1,0:T(8,128)(2,1)}), bf16[16,64,256]{2,1,0:T(8,128)(2,1)S(1)}, u32[]{:S(2)}, u32[]{:S(2)}) async-start(bf16[16,64,256]{2,1,0:T(8,128)(2,1)} %shard_map.92), calls=%async_computation.1 | async-start | bytes 1048576 | tf_op jit(solution)/shard_map/all_to_all | solution.py:245
  104.0 32.6 %collective-permute-start.13 = (bf16[4,512,256]{2,1,0:T(8,128)(2,1)S(1)}, bf16[4,512,256]{2,1,0:T(8,128)(2,1)}, u32[]{:S(2)}, u32[]{:S(2)}) collective-permute-start(bf16[4,512,256]{2,1,0:T(8,128)(2,1)S(1)} %copy-done.10), channel_id=1, source_target_pairs={{0,1},{1,0},{2,3},{3,2},{4,5},{5,4},{6,7},{7,6},{8,9},{9,8},{10,11... | collective-permute-start | bytes 3145736 | tf_op jit(solution)/shard_map/ppermute | solution.py:325
  118.8 23.5 %all-to-all-start.2 = ((bf16[16,64,256]{2,1,0:T(8,128)(2,1)}), bf16[16,64,256]{2,1,0:T(8,128)(2,1)S(1)}, u32[]{:S(2)}, u32[]{:S(2)}) async-start(bf16[16,64,256]{2,1,0:T(8,128)(2,1)} %bitcast.8), calls=%async_computation.2 | async-start | bytes 1048576 | tf_op jit(solution)/shard_map/all_to_all | solution.py:235
  125.0 11.6 %copy-start.21 = (bf16[4,512,256]{2,1,0:T(8,128)(2,1)S(1)}, bf16[4,512,256]{2,1,0:T(8,128)(2,1)}, u32[]{:S(2)}) copy-start(bf16[4,512,256]{2,1,0:T(8,128)(2,1)} %copy-done.20) | copy-start | bytes 3145732
  125.9 14.7 %collective-permute-start.14 = (f32[128,256]{1,0:T(8,128)S(1)}, f32[128,256]{1,0:T(8,128)S(1)}, u32[]{:S(2)}, u32[]{:S(2)}) collective-permute-start(f32[128,256]{1,0:T(8,128)S(1)} %get-tuple-element.77), channel_id=1, source_target_pairs={{0,1},{1,0},{2,3},{3,2},{4,5},{5,4},{6,7},{7,6},{8,9},{9,8},{10,11... | collective-permute-start | bytes 393224 | tf_op jit(solution)/shard_map/ppermute | solution.py:330
  (16 other events, 38.4 us)

commit v4 on v3

--- a/solution.py
+++ b/solution.py
@@ -132,30 +132,19 @@
 
 
 def join_kernel(here, mine, other, out):
-    n = mine.shape[1] // 2
-    total = mine[0].astype(F32) + other[0].astype(F32)
+    n, rows, width = mine.shape
     even = here[1] == 0
-    out[:, :n] = jnp.where(even, total[:n], total[n:]).astype(BF16)
-    out[:, n:] = jnp.where(even, total[n:], total[:n]).astype(BF16)
+    for i in range(n):
+        total = mine[i].astype(F32) + other[i].astype(F32)
+        top, bottom = total[: rows // 2], total[rows // 2 :]
+        out[:, 2 * i * width : (2 * i + 1) * width] = jnp.where(even, top, bottom).astype(BF16)
+        out[:, (2 * i + 1) * width : (2 * i + 2) * width] = jnp.where(even, bottom, top).astype(BF16)
 
 
 def join(here, mine, other):
-    n, rows, width = other.shape
-    return pl.pallas_call(
-        join_kernel,
-        grid_spec=pltpu.PrefetchScalarGridSpec(
-            num_scalar_prefetch=1,
-            grid=(n,),
-            in_specs=[
-                pl.BlockSpec((1, rows, width), lambda i, p: (i, 0, 0)),
-                pl.BlockSpec((1, rows, width), lambda i, p: (i, 0, 0)),
-            ],
-            out_specs=pl.BlockSpec((rows // 2, 2 * width), lambda i, p: (0, i)),
-        ),
-        out_shape=jax.ShapeDtypeStruct((rows // 2, 2 * n * width), BF16),
-        compiler_params=pltpu.CompilerParams(vmem_limit_bytes=VMEM_BYTES),
-        cost_estimate=cost(4),
-    )(here, mine, other)
+    n, rows, width = mine.shape
+    out_shape = jax.ShapeDtypeStruct((rows // 2, 2 * n * width), BF16)
+    return kernel_call(join_kernel, [here, mine, other], out_shape, 2)
 
 
 def prologue_kernel(block, mask_ref, pre_ref, lat_ref, lat_t_ref):
@@ -312,13 +301,12 @@
         blocks.append(dec)
         blocks_s.append(dec_s)
         x, y = nx, ny
-    x, total, total_s, dec_s = lax.optimization_barrier((x, total, total_s, dec_s))
     received = lax.ppermute(total_s, "lat", swap)
+    x, total, dec_s = lax.optimization_barrier((x, total, dec_s))
+    dec_got = lax.ppermute(dec_s, "lat", swap)
     y = lax.ppermute(x, "lat", swap)
     grad_part = finish(here, x, y, weights, total, received, latents)
 
-    grad_part, dec_s = lax.optimization_barrier((grad_part, dec_s))
-    dec_got = lax.ppermute(dec_s, "lat", swap)
     terms = exchange(grad_part, "tgt")
     keep, send = place(here, x, y, lat_t, dec_got, blocks)
     terms, send = lax.optimization_barrier((terms, send))
@@ -330,7 +318,7 @@
     enc_other = lax.ppermute(enc_send, "tok", tok_swap)
     dec_grad = join(here, keep, other)[None]
     enc_grad = enc_keep + enc_other
-    terms, dec_grad, enc_grad = lax.optimization_barrier((terms, dec_grad, enc_grad))
+    terms, dec_grad = lax.optimization_barrier((terms, dec_grad))
     input_grad = lax.all_gather(sum_part(terms), "lat", axis=0, tiled=True)
     return (dec_grad, enc_grad, input_grad)
 

time: 162 us -> 156 us (0.963)
  waiting for transfers between devices: 32.8 us -> 28.1 us
    pallas_call x1 -> x0, Pallas kernels: 4.03 us -> none  [join(): pl.pallas_call(join_kernel, grid_spec=pltpu.PrefetchScalarGridSpec(num_sc...]
    pallas_call x7 -> x8, Pallas kernels: 13.4 us -> 16.2 us  [kernel_call(): pl.pallas_call(body, in_specs=[SMEM] + [VMEM] * (len(args) - 1), out_spec...]
    ppermute x3, waiting for transfers between devices: 2 us -> 0.01 us  [shards(): nx = lax.ppermute(x, 'lat', ring)]
    ppermute x1, waiting for transfers between devices: 1.88 us -> 0.01 us  [shards(): y = lax.ppermute(x, 'lat', swap)]
    unnamed x45 -> x49, local copies, waits for them, and re-layouts: 12.8 us -> 12.8 us
  transfers between devices with their start and end apart: 18 -> 18, of which waited for: 8 -> 7; matrix products, arithmetic and copies ran while one was open for 0% -> 0% of each run, Pallas kernels for 11% -> 12%
where the time goes in v4:
time: 156 us; the launch traced here: 155 us
  starting transfers between devices  76.3 us (49%)
  waiting for transfers between devices  28.1 us (18%)
  Pallas kernels  19.4 us (12%)
  blocking collectives  16.7 us (11%)
  local copies, waits for them, and re-layouts  12.8 us (8%)
    all_gather x1, blocking collectives, shards(): input_grad = lax.all_gather(sum_part(terms), 'lat', axis=0, tiled=True)  16.7 us
    pallas_call x8, Pallas kernels, kernel_call(): pl.pallas_call(body, in_specs=[SMEM] + [VMEM] * (len(args) - 1), out_spec...  16.2 us
    all_to_all x2, starting transfers between devices, exchange(): lax.all_to_all(terms.reshape(n, terms.shape[0] // n, terms.shape[1]), axi...  14.7 us
    unnamed x49, local copies, waits for them, and re-layouts  12.8 us
    ppermute x3, starting transfers between devices, shards(): nx = lax.ppermute(x, 'lat', ring)  11 us
    ppermute x1, starting transfers between devices, shards(): lax.ppermute(weights, 'lat', swap)  8.79 us
    all_to_all x1, waiting for transfers between devices, spread(): return lax.all_to_all(copies, axis, 0, 0).reshape(-1, got.shape[2])  8.4 us
    all_to_all x2, waiting for transfers between devices, exchange(): lax.all_to_all(terms.reshape(n, terms.shape[0] // n, terms.shape[1]), axi...  7.99 us
  transfers between devices with their start and end apart: 18, of which 7 were waited for; matrix products, arithmetic and copies ran while one was open for 0% of the time, Pallas kernels for 12%

profile of v4, /device:TPU:1, one launch (start us, length us, event | category | flops | bytes accessed | tf_op | source)
XLA Modules:
  0.0 155.1 jit_solution(6176329871459782349)
XLA Ops:
  0.6 8.8 %collective-permute-start.1 = (bf16[256,4096]{1,0:T(8,128)(2,1)}, bf16[256,4096]{1,0:T(8,128)(2,1)S(1)}, u32[]{:S(2)}, u32[]{:S(2)}) collective-permute-start(bf16[256,4096]{1,0:T(8,128)(2,1)} %bitcast.10), channel_id=1, source_target_pairs={{0,32},{32,0},{64,96},{96,64},{128,160},{160,128},{192,224},{224,1... | collective-permute-start | bytes 6291464 | tf_op jit(solution)/shard_map/ppermute | solution.py:280
  9.4 5.3 %collective-permute-start = (bf16[1024,256]{1,0:T(8,128)(2,1)}, bf16[1024,256]{1,0:T(8,128)(2,1)}, u32[]{:S(2)}, u32[]{:S(2)}) collective-permute-start(bf16[1024,256]{1,0:T(8,128)(2,1)} %bitcast.18), channel_id=1, source_target_pairs={{0,64},{32,480},{64,128},{96,32},{128,192},{160,96},{192,256},{224... | collective-permute-start | bytes 1572872 | tf_op jit(solution)/shard_map/ppermute | solution.py:282
  23.6 4.9 %collective-permute-start.3 = (bf16[1024,256]{1,0:T(8,128)(2,1)}, bf16[1024,256]{1,0:T(8,128)(2,1)}, u32[]{:S(2)}, u32[]{:S(2)}) collective-permute-start(bf16[1024,256]{1,0:T(8,128)(2,1)} %collective-permute-done.refs_0_), channel_id=1, source_target_pairs={{0,64},{32,480},{64,128},{96,32},{128,192},{160,96},{192,256},{224... | collective-permute-start | bytes 1572872 | tf_op jit(solution)/shard_map/ppermute | solution.py:292
  28.5 5.3 %collective-permute-done.4.refs_1_ = bf16[1024,256]{1,0:T(8,128)(2,1)} collective-permute-done((bf16[1024,256]{1,0:T(8,128)(2,1)S(1)}, bf16[1024,256]{1,0:T(8,128)(2,1)}, u32[]{:S(2)}, u32[]{:S(2)}) %collective-permute-start.4) | collective-permute-done | bytes 524320 | tf_op jit(solution)/shard_map/ppermute | solution.py:281
  37.4 2.5 %shard_map.86 = (f32[1024,256]{1,0:T(8,128)S(1)}, bf16[512,256]{1,0:T(8,128)(2,1)S(1)}, f32[1024,256]{1,0:T(8,128)S(1)}, bf16[512,256]{1,0:T(8,128)(2,1)S(1)}) custom-call(s32[3]{0:T(128)S(1)} %pad_add_fusion.here, bf16[1024,256]{1,0:T(8,128)(2,1)} %collective-permute-done.refs_0_, bf16[1024,256]{1,0:T(8,128)(2,1)} %collective-permute-done.4.refs_1_, ...), custom_call_target="tpu_custom_call" | custom-call | flops 1000000000 | bytes 8912908 | tf_op jit(solution)/shard_map/pallas_call | solution.py:65
  40.0 2.3 %collective-permute-start.5 = (bf16[1024,256]{1,0:T(8,128)(2,1)}, bf16[1024,256]{1,0:T(8,128)(2,1)S(1)}, u32[]{:S(2)}, u32[]{:S(2)}) collective-permute-start(bf16[1024,256]{1,0:T(8,128)(2,1)} %collective-permute-done.3.refs_0_), channel_id=1, source_target_pairs={{0,64},{32,480},{64,128},{96,32},{128,192},{160,96},{192,256},{224... | collective-permute-start | bytes 1572872 | tf_op jit(solution)/shard_map/ppermute | solution.py:292
  44.3 4.5 %collective-permute-start.8 = (bf16[1024,256]{1,0:T(8,128)(2,1)}, bf16[1024,256]{1,0:T(8,128)(2,1)S(1)}, u32[]{:S(2)}, u32[]{:S(2)}) collective-permute-start(bf16[1024,256]{1,0:T(8,128)(2,1)} %collective-permute-done.6.refs_1_), channel_id=1, source_target_pairs={{0,64},{32,480},{64,128},{96,32},{128,192},{160,96},{192,256},{224... | collective-permute-start | bytes 1572872 | tf_op jit(solution)/shard_map/ppermute | solution.py:293
  48.8 2.5 %shard_map.87 = (f32[1024,256]{1,0:T(8,128)S(1)}, bf16[512,256]{1,0:T(8,128)(2,1)S(1)}, f32[1024,256]{1,0:T(8,128)S(1)}, bf16[512,256]{1,0:T(8,128)(2,1)S(1)}) custom-call(s32[3]{0:T(128)S(1)} %pad_add_fusion.here, bf16[1024,256]{1,0:T(8,128)(2,1)} %collective-permute-done.3.refs_0_, bf16[1024,256]{1,0:T(8,128)(2,1)} %collective-permute-done.6.refs_1_, ...), custom_call_target="tpu_custom_call" | custom-call | flops 1000000000 | bytes 11010060 | tf_op jit(solution)/shard_map/pallas_call | solution.py:65
  52.0 3.8 %collective-permute-start.7 = (bf16[1024,256]{1,0:T(8,128)(2,1)S(1)}, bf16[1024,256]{1,0:T(8,128)(2,1)S(1)}, u32[]{:S(2)}, u32[]{:S(2)}) collective-permute-start(bf16[1024,256]{1,0:T(8,128)(2,1)S(1)} %collective-permute-done.5.refs_0_), channel_id=1, source_target_pairs={{0,64},{32,480},{64,128},{96,32},{128,192},{160,96},{192,256},{224... | collective-permute-start | bytes 1572872 | tf_op jit(solution)/shard_map/ppermute | solution.py:292
  57.1 2.7 %shard_map.89 = (f32[1024,256]{1,0:T(8,128)S(1)}, bf16[512,256]{1,0:T(8,128)(2,1)S(1)}, f32[1024,256]{1,0:T(8,128)S(1)}, bf16[3,512,256]{2,1,0:T(8,128)(2,1)}) custom-call(s32[3]{0:T(128)S(1)} %pad_add_fusion.here, bf16[1024,256]{1,0:T(8,128)(2,1)S(1)} %collective-permute-done.5.refs_0_, bf16[1024,256]{1,0:T(8,128)(2,1)S(1)} %collective-permute-done.8.refs_1_, ...), custom_call_target="tpu_custom_call" | custom-call | flops 1000000000 | bytes 12058636 | tf_op jit(solution)/shard_map/pallas_call | solution.py:65
  59.9 3.7 %collective-permute-start.11 = (f32[1024,256]{1,0:T(8,128)S(1)}, f32[1024,256]{1,0:T(8,128)S(1)}, u32[]{:S(2)}, u32[]{:S(2)}) collective-permute-start(f32[1024,256]{1,0:T(8,128)S(1)} %get-tuple-element.58), channel_id=1, source_target_pairs={{0,32},{32,0},{64,96},{96,64},{128,160},{160,128},{192,224},{224,1... | collective-permute-start | bytes 3145736 | tf_op jit(solution)/shard_map/ppermute | solution.py:304
  63.7 3.2 %collective-permute-start.10 = (bf16[1024,256]{1,0:T(8,128)(2,1)S(1)}, bf16[1024,256]{1,0:T(8,128)(2,1)S(1)}, u32[]{:S(2)}, u32[]{:S(2)}) collective-permute-start(bf16[1024,256]{1,0:T(8,128)(2,1)S(1)} %collective-permute-done.7.ex), channel_id=1, source_target_pairs={{0,32},{32,0},{64,96},{96,64},{128,160},{160,128},{192,224},{224,1... | collective-permute-start | bytes 1572872 | tf_op jit(solution)/shard_map/ppermute | solution.py:307
  66.9 1.9 %collective-permute-start.12 = (bf16[3,512,256]{2,1,0:T(8,128)(2,1)}, bf16[3,512,256]{2,1,0:T(8,128)(2,1)}, u32[]{:S(2)}, u32[]{:S(2)}) collective-permute-start(bf16[3,512,256]{2,1,0:T(8,128)(2,1)} %get-tuple-element.60), channel_id=1, source_target_pairs={{0,32},{32,0},{64,96},{96,64},{128,160},{160,128},{192,224},{224,1... | collective-permute-start | bytes 2359304 | tf_op jit(solution)/shard_map/ppermute | solution.py:306
  70.7 7.9 %all-to-all-start = ((bf16[16,64,256]{2,1,0:T(8,128)(2,1)}), bf16[16,64,256]{2,1,0:T(8,128)(2,1)S(1)}, u32[]{:S(2)}, u32[]{:S(2)}) async-start(bf16[16,64,256]{2,1,0:T(8,128)(2,1)} %bitcast.6), calls=%async_computation | async-start | bytes 1048576 | tf_op jit(solution)/shard_map/all_to_all | solution.py:224
  86.4 5.5 %all-to-all-done.got = bf16[16,64,256]{2,1,0:T(8,128)(2,1)S(1)} async-done(((bf16[16,64,256]{2,1,0:T(8,128)(2,1)}), bf16[16,64,256]{2,1,0:T(8,128)(2,1)S(1)}, u32[]{:S(2)}, u32[]{:S(2)}) %all-to-all-start) | async-done | bytes 524320 | tf_op jit(solution)/shard_map/all_to_all | solution.py:224
  92.7 6.7 %all-to-all-start.1 = ((bf16[16,64,256]{2,1,0:T(8,128)(2,1)}), bf16[16,64,256]{2,1,0:T(8,128)(2,1)S(1)}, u32[]{:S(2)}, u32[]{:S(2)}) async-start(bf16[16,64,256]{2,1,0:T(8,128)(2,1)} %shard_map.92), calls=%async_computation.1 | async-start | bytes 1048576 | tf_op jit(solution)/shard_map/all_to_all | solution.py:234
  99.4 4.4 %collective-permute-start.13 = (bf16[4,512,256]{2,1,0:T(8,128)(2,1)S(1)}, bf16[4,512,256]{2,1,0:T(8,128)(2,1)}, u32[]{:S(2)}, u32[]{:S(2)}) collective-permute-start(bf16[4,512,256]{2,1,0:T(8,128)(2,1)S(1)} %copy-done.12), channel_id=1, source_target_pairs={{0,1},{1,0},{2,3},{3,2},{4,5},{5,4},{6,7},{7,6},{8,9},{9,8},{10,11... | collective-permute-start | bytes 3145736 | tf_op jit(solution)/shard_map/ppermute | solution.py:313
  103.8 8.4 %all-to-all-done.1 = bf16[16,64,256]{2,1,0:T(8,128)(2,1)S(1)} async-done(((bf16[16,64,256]{2,1,0:T(8,128)(2,1)}), bf16[16,64,256]{2,1,0:T(8,128)(2,1)S(1)}, u32[]{:S(2)}, u32[]{:S(2)}) %all-to-all-start.1) | async-done | bytes 524320 | tf_op jit(solution)/shard_map/all_to_all | solution.py:234
  113.3 6.9 %all-to-all-start.2 = ((bf16[16,64,256]{2,1,0:T(8,128)(2,1)}), bf16[16,64,256]{2,1,0:T(8,128)(2,1)S(1)}, u32[]{:S(2)}, u32[]{:S(2)}) async-start(bf16[16,64,256]{2,1,0:T(8,128)(2,1)} %bitcast.8), calls=%async_computation.2 | async-start | bytes 1048576 | tf_op jit(solution)/shard_map/all_to_all | solution.py:224
  121.1 4.4 %collective-permute-start.14 = (f32[128,256]{1,0:T(8,128)S(1)}, f32[128,256]{1,0:T(8,128)S(1)}, u32[]{:S(2)}, u32[]{:S(2)}) collective-permute-start(f32[128,256]{1,0:T(8,128)S(1)} %get-tuple-element.71), channel_id=1, source_target_pairs={{0,1},{1,0},{2,3},{3,2},{4,5},{5,4},{6,7},{7,6},{8,9},{9,8},{10,11... | collective-permute-start | bytes 393224 | tf_op jit(solution)/shard_map/ppermute | solution.py:318
  125.5 6.2 %collective-permute-done.13.other = bf16[4,512,256]{2,1,0:T(8,128)(2,1)} collective-permute-done((bf16[4,512,256]{2,1,0:T(8,128)(2,1)S(1)}, bf16[4,512,256]{2,1,0:T(8,128)(2,1)}, u32[]{:S(2)}, u32[]{:S(2)}) %collective-permute-start.13) | collective-permute-done | bytes 1048608 | tf_op jit(solution)/shard_map/ppermute | solution.py:313
  131.7 2.5 %shard_map.94 = bf16[256,2048]{1,0:T(8,128)(2,1)} custom-call(s32[3]{0:T(128)S(1)} %pad_add_fusion.here, bf16[4,512,256]{2,1,0:T(8,128)(2,1)S(1)} %copy-done.23, bf16[4,512,256]{2,1,0:T(8,128)(2,1)} %collective-permute-done.13.other), custom_call_target="tpu_custom_call" | custom-call | flops 2000000000 | bytes 3145740 | tf_op jit(solution)/shard_map/pallas_call | solution.py:65
  135.0 2.5 %all-to-all-done.2.got = bf16[16,64,256]{2,1,0:T(8,128)(2,1)S(1)} async-done(((bf16[16,64,256]{2,1,0:T(8,128)(2,1)}), bf16[16,64,256]{2,1,0:T(8,128)(2,1)S(1)}, u32[]{:S(2)}, u32[]{:S(2)}) %all-to-all-start.2) | async-done | bytes 524320 | tf_op jit(solution)/shard_map/all_to_all | solution.py:224
  137.6 16.7 %all_gather.3 = bf16[1024,256]{1,0:T(8,128)(2,1)S(1)} all-gather(bf16[64,256]{1,0:T(8,128)(2,1)S(1)} %shard_map.96), channel_id=1, replica_groups=mesh['lat'=16,'tgt'=16,'tok'=2] {'lat'}, dimensions={0}, use_global_device_ids=true | all-gather | bytes 557056 | tf_op jit(solution)/shard_map/all_gather | solution.py:322
  (76 shorter events, 30.6 us)
Async XLA Ops:
  0.6 21.6 %collective-permute-start.1 = (bf16[256,4096]{1,0:T(8,128)(2,1)}, bf16[256,4096]{1,0:T(8,128)(2,1)S(1)}, u32[]{:S(2)}, u32[]{:S(2)}) collective-permute-start(bf16[256,4096]{1,0:T(8,128)(2,1)} %bitcast.10), channel_id=1, source_target_pairs={{0,32},{32,0},{64,96},{96,64},{128,160},{160,128},{192,224},{224,1... | collective-permute-start | bytes 6291464 | tf_op jit(solution)/shard_map/ppermute | solution.py:280
  9.4 12.8 %collective-permute-start = (bf16[1024,256]{1,0:T(8,128)(2,1)}, bf16[1024,256]{1,0:T(8,128)(2,1)}, u32[]{:S(2)}, u32[]{:S(2)}) collective-permute-start(bf16[1024,256]{1,0:T(8,128)(2,1)} %bitcast.18), channel_id=1, source_target_pairs={{0,64},{32,480},{64,128},{96,32},{128,192},{160,96},{192,256},{224... | collective-permute-start | bytes 1572872 | tf_op jit(solution)/shard_map/ppermute | solution.py:282
  16.5 19.4 %copy-start = (bf16[1,256,4096]{2,1,0:T(8,128)(2,1)S(1)}, bf16[1,256,4096]{2,1,0:T(8,128)(2,1)}, u32[]{:S(2)}) copy-start(bf16[1,256,4096]{2,1,0:T(8,128)(2,1)} %param.7) | copy-start | bytes 6291460
  18.4 3.9 %collective-permute-start.2 = (bf16[256,1024]{1,0:T(8,128)(2,1)S(1)}, bf16[256,1024]{1,0:T(8,128)(2,1)S(1)}, u32[]{:S(2)}, u32[]{:S(2)}) collective-permute-start(bf16[256,1024]{1,0:T(8,128)(2,1)S(1)} %get-tuple-element.38.refs_3_.lat_t), channel_id=1, source_target_pairs={{0,32},{32,0},{64,96},{96,64},{128,160},{160,128},{192,224},{224,1... | collective-permute-start | bytes 1572872 | tf_op jit(solution)/shard_map/ppermute | solution.py:280
  20.3 13.5 %collective-permute-start.4 = (bf16[1024,256]{1,0:T(8,128)(2,1)S(1)}, bf16[1024,256]{1,0:T(8,128)(2,1)}, u32[]{:S(2)}, u32[]{:S(2)}) collective-permute-start(bf16[1024,256]{1,0:T(8,128)(2,1)S(1)} %bitcast.19), channel_id=1, source_target_pairs={{0,480},{32,64},{64,32},{96,128},{128,96},{160,192},{192,160},{224... | collective-permute-start | bytes 1572872 | tf_op jit(solution)/shard_map/ppermute | solution.py:281
  23.6 16.4 %collective-permute-start.3 = (bf16[1024,256]{1,0:T(8,128)(2,1)}, bf16[1024,256]{1,0:T(8,128)(2,1)}, u32[]{:S(2)}, u32[]{:S(2)}) collective-permute-start(bf16[1024,256]{1,0:T(8,128)(2,1)} %collective-permute-done.refs_0_), channel_id=1, source_target_pairs={{0,64},{32,480},{64,128},{96,32},{128,192},{160,96},{192,256},{224... | collective-permute-start | bytes 1572872 | tf_op jit(solution)/shard_map/ppermute | solution.py:292
  33.8 10.5 %collective-permute-start.6 = (bf16[1024,256]{1,0:T(8,128)(2,1)}, bf16[1024,256]{1,0:T(8,128)(2,1)}, u32[]{:S(2)}, u32[]{:S(2)}) collective-permute-start(bf16[1024,256]{1,0:T(8,128)(2,1)} %collective-permute-done.4.refs_1_), channel_id=1, source_target_pairs={{0,64},{32,480},{64,128},{96,32},{128,192},{160,96},{192,256},{224... | collective-permute-start | bytes 1572872 | tf_op jit(solution)/shard_map/ppermute | solution.py:293
  40.0 12.1 %collective-permute-start.5 = (bf16[1024,256]{1,0:T(8,128)(2,1)}, bf16[1024,256]{1,0:T(8,128)(2,1)S(1)}, u32[]{:S(2)}, u32[]{:S(2)}) collective-permute-start(bf16[1024,256]{1,0:T(8,128)(2,1)} %collective-permute-done.3.refs_0_), channel_id=1, source_target_pairs={{0,64},{32,480},{64,128},{96,32},{128,192},{160,96},{192,256},{224... | collective-permute-start | bytes 1572872 | tf_op jit(solution)/shard_map/ppermute | solution.py:292
  42.3 13.5 %collective-permute-start.9 = (bf16[1024,256]{1,0:T(8,128)(2,1)S(1)}, bf16[1024,256]{1,0:T(8,128)(2,1)S(1)}, u32[]{:S(2)}, u32[]{:S(2)}) collective-permute-start(bf16[1024,256]{1,0:T(8,128)(2,1)S(1)} %bitcast.20), channel_id=1, source_target_pairs={{0,32},{32,0},{64,96},{96,64},{128,160},{160,128},{192,224},{224,1... | collective-permute-start | bytes 1572872 | tf_op jit(solution)/shard_map/ppermute | solution.py:289
  44.3 12.8 %collective-permute-start.8 = (bf16[1024,256]{1,0:T(8,128)(2,1)}, bf16[1024,256]{1,0:T(8,128)(2,1)S(1)}, u32[]{:S(2)}, u32[]{:S(2)}) collective-permute-start(bf16[1024,256]{1,0:T(8,128)(2,1)} %collective-permute-done.6.refs_1_), channel_id=1, source_target_pairs={{0,64},{32,480},{64,128},{96,32},{128,192},{160,96},{192,256},{224... | collective-permute-start | bytes 1572872 | tf_op jit(solution)/shard_map/ppermute | solution.py:293
  52.0 11.6 %collective-permute-start.7 = (bf16[1024,256]{1,0:T(8,128)(2,1)S(1)}, bf16[1024,256]{1,0:T(8,128)(2,1)S(1)}, u32[]{:S(2)}, u32[]{:S(2)}) collective-permute-start(bf16[1024,256]{1,0:T(8,128)(2,1)S(1)} %collective-permute-done.5.refs_0_), channel_id=1, source_target_pairs={{0,64},{32,480},{64,128},{96,32},{128,192},{160,96},{192,256},{224... | collective-permute-start | bytes 1572872 | tf_op jit(solution)/shard_map/ppermute | solution.py:292
  57.1 11.7 %copy-start.7 = (bf16[1024,256]{1,0:T(8,128)(2,1)S(1)}, bf16[1024,256]{1,0:T(8,128)(2,1)}, u32[]{:S(2)}) copy-start(bf16[1024,256]{1,0:T(8,128)(2,1)} %copy-done.6) | copy-start | bytes 1572868
  59.9 10.9 %copy-start.19 = (bf16[512,256]{1,0:T(8,128)(2,1)}, bf16[512,256]{1,0:T(8,128)(2,1)S(1)}, u32[]{:S(2)}) copy-start(bf16[512,256]{1,0:T(8,128)(2,1)S(1)} %get-tuple-element.64.refs_3_) | copy-start | bytes 786436
  59.9 9.0 %collective-permute-start.11 = (f32[1024,256]{1,0:T(8,128)S(1)}, f32[1024,256]{1,0:T(8,128)S(1)}, u32[]{:S(2)}, u32[]{:S(2)}) collective-permute-start(f32[1024,256]{1,0:T(8,128)S(1)} %get-tuple-element.58), channel_id=1, source_target_pairs={{0,32},{32,0},{64,96},{96,64},{128,160},{160,128},{192,224},{224,1... | collective-permute-start | bytes 3145736 | tf_op jit(solution)/shard_map/ppermute | solution.py:304
  63.7 5.2 %collective-permute-start.10 = (bf16[1024,256]{1,0:T(8,128)(2,1)S(1)}, bf16[1024,256]{1,0:T(8,128)(2,1)S(1)}, u32[]{:S(2)}, u32[]{:S(2)}) collective-permute-start(bf16[1024,256]{1,0:T(8,128)(2,1)S(1)} %collective-permute-done.7.ex), channel_id=1, source_target_pairs={{0,32},{32,0},{64,96},{96,64},{128,160},{160,128},{192,224},{224,1... | collective-permute-start | bytes 1572872 | tf_op jit(solution)/shard_map/ppermute | solution.py:307
  66.9 11.7 %collective-permute-start.12 = (bf16[3,512,256]{2,1,0:T(8,128)(2,1)}, bf16[3,512,256]{2,1,0:T(8,128)(2,1)}, u32[]{:S(2)}, u32[]{:S(2)}) collective-permute-start(bf16[3,512,256]{2,1,0:T(8,128)(2,1)} %get-tuple-element.60), channel_id=1, source_target_pairs={{0,32},{32,0},{64,96},{96,64},{128,160},{160,128},{192,224},{224,1... | collective-permute-start | bytes 2359304 | tf_op jit(solution)/shard_map/ppermute | solution.py:306
  70.7 21.1 %all-to-all-start = ((bf16[16,64,256]{2,1,0:T(8,128)(2,1)}), bf16[16,64,256]{2,1,0:T(8,128)(2,1)S(1)}, u32[]{:S(2)}, u32[]{:S(2)}) async-start(bf16[16,64,256]{2,1,0:T(8,128)(2,1)} %bitcast.6), calls=%async_computation | async-start | bytes 1048576 | tf_op jit(solution)/shard_map/all_to_all | solution.py:224
  86.4 25.8 %copy-start.10 = (bf16[256,256]{1,0:T(8,128)(2,1)S(1)}, bf16[256,256]{1,0:T(8,128)(2,1)}, u32[]{:S(2)}) copy-start(bf16[256,256]{1,0:T(8,128)(2,1)} %encoder.1) | copy-start | bytes 393220
  91.8 28.4 %copy-start.14 = (bf16[1024,256]{1,0:T(8,128)(2,1)S(1)}, bf16[1024,256]{1,0:T(8,128)(2,1)}, u32[]{:S(2)}) copy-start(bf16[1024,256]{1,0:T(8,128)(2,1)} %inputs.1) | copy-start | bytes 1572868
  92.7 19.5 %all-to-all-start.1 = ((bf16[16,64,256]{2,1,0:T(8,128)(2,1)}), bf16[16,64,256]{2,1,0:T(8,128)(2,1)S(1)}, u32[]{:S(2)}, u32[]{:S(2)}) async-start(bf16[16,64,256]{2,1,0:T(8,128)(2,1)} %shard_map.92), calls=%async_computation.1 | async-start | bytes 1048576 | tf_op jit(solution)/shard_map/all_to_all | solution.py:234
  99.4 32.2 %collective-permute-start.13 = (bf16[4,512,256]{2,1,0:T(8,128)(2,1)S(1)}, bf16[4,512,256]{2,1,0:T(8,128)(2,1)}, u32[]{:S(2)}, u32[]{:S(2)}) collective-permute-start(bf16[4,512,256]{2,1,0:T(8,128)(2,1)S(1)} %copy-done.12), channel_id=1, source_target_pairs={{0,1},{1,0},{2,3},{3,2},{4,5},{5,4},{6,7},{7,6},{8,9},{9,8},{10,11... | collective-permute-start | bytes 3145736 | tf_op jit(solution)/shard_map/ppermute | solution.py:313
  113.3 24.2 %all-to-all-start.2 = ((bf16[16,64,256]{2,1,0:T(8,128)(2,1)}), bf16[16,64,256]{2,1,0:T(8,128)(2,1)S(1)}, u32[]{:S(2)}, u32[]{:S(2)}) async-start(bf16[16,64,256]{2,1,0:T(8,128)(2,1)} %bitcast.8), calls=%async_computation.2 | async-start | bytes 1048576 | tf_op jit(solution)/shard_map/all_to_all | solution.py:224
  120.2 11.4 %copy-start.23 = (bf16[4,512,256]{2,1,0:T(8,128)(2,1)S(1)}, bf16[4,512,256]{2,1,0:T(8,128)(2,1)}, u32[]{:S(2)}) copy-start(bf16[4,512,256]{2,1,0:T(8,128)(2,1)} %copy-done.22) | copy-start | bytes 3145732
  121.1 13.2 %collective-permute-start.14 = (f32[128,256]{1,0:T(8,128)S(1)}, f32[128,256]{1,0:T(8,128)S(1)}, u32[]{:S(2)}, u32[]{:S(2)}) collective-permute-start(f32[128,256]{1,0:T(8,128)S(1)} %get-tuple-element.71), channel_id=1, source_target_pairs={{0,1},{1,0},{2,3},{3,2},{4,5},{5,4},{6,7},{7,6},{8,9},{9,8},{10,11... | collective-permute-start | bytes 393224 | tf_op jit(solution)/shard_map/ppermute | solution.py:318
  (18 other events, 43.3 us)

commit v5 on v4

--- a/solution.py
+++ b/solution.py
@@ -147,39 +147,23 @@
     return kernel_call(join_kernel, [here, mine, other], out_shape, 2)
 
 
-def prologue_kernel(block, mask_ref, pre_ref, lat_ref, lat_t_ref):
-    first = pl.program_id(0) * (pre_ref.shape[0] // block)
-    for i in range(pre_ref.shape[0] // block):
-        for j in range(pre_ref.shape[1] // block):
+def prologue_kernel(mask, pre_ref, lat_ref, lat_t_ref):
+    block = pre_ref.shape[0] // mask.shape[1]
+    for i in range(mask.shape[1]):
+        for j in range(mask.shape[0]):
             at = (pl.ds(i * block, block), pl.ds(j * block, block))
             value = jnp.maximum(pre_ref[at].astype(F32), 0.0)
-            value = jnp.where(mask_ref[j, first + i] > 0, value, 0.0)
+            value = jnp.where(mask[j, i] > 0, value, 0.0)
             lat_ref[at] = value.astype(BF16)
             lat_t_ref[at[1], at[0]] = value.T.astype(BF16)
 
 
 def prologue(block_mask, pre_acts):
-    tokens, rows = pre_acts.shape
-    block = tokens // block_mask.shape[0]
-    n = 4
-    return pl.pallas_call(
-        functools.partial(prologue_kernel, block),
-        grid_spec=pltpu.PrefetchScalarGridSpec(
-            num_scalar_prefetch=1,
-            grid=(n,),
-            in_specs=[pl.BlockSpec((tokens // n, rows), lambda i, p: (i, 0))],
-            out_specs=[
-                pl.BlockSpec((tokens // n, rows), lambda i, p: (i, 0)),
-                pl.BlockSpec((rows, tokens // n), lambda i, p: (0, i)),
-            ],
-        ),
-        out_shape=[
-            jax.ShapeDtypeStruct((tokens, rows), BF16),
-            jax.ShapeDtypeStruct((rows, tokens), BF16),
-        ],
-        compiler_params=pltpu.CompilerParams(vmem_limit_bytes=VMEM_BYTES),
-        cost_estimate=cost(4),
-    )(block_mask.T, pre_acts)
+    out_shape = [
+        jax.ShapeDtypeStruct(pre_acts.shape, BF16),
+        jax.ShapeDtypeStruct(pre_acts.shape[::-1], BF16),
+    ]
+    return kernel_call(prologue_kernel, [block_mask.T, pre_acts], out_shape, 4)
 
 
 def finish_kernel(here, ex, ey, weights, total, received, live, out):

time: 156 us -> 156 us (level)
    pallas_call x8 -> x9, Pallas kernels: 16.2 us -> 17.1 us  [kernel_call(): pl.pallas_call(body, in_specs=[SMEM] + [VMEM] * (len(args) - 1), out_spec...]
where the time goes in v5:
time: 156 us; the launch traced here: 155 us
  starting transfers between devices  76.3 us (49%)
  waiting for transfers between devices  28.1 us (18%)
  Pallas kernels  19.1 us (12%)
  blocking collectives  16.7 us (11%)
  local copies, waits for them, and re-layouts  12.8 us (8%)
    pallas_call x9, Pallas kernels, kernel_call(): pl.pallas_call(body, in_specs=[SMEM] + [VMEM] * (len(args) - 1), out_spec...  17.1 us
    all_gather x1, blocking collectives, shards(): input_grad = lax.all_gather(sum_part(terms), 'lat', axis=0, tiled=True)  16.7 us
    all_to_all x2, starting transfers between devices, exchange(): lax.all_to_all(terms.reshape(n, terms.shape[0] // n, terms.shape[1]), axi...  14.7 us
    unnamed x49, local copies, waits for them, and re-layouts  12.8 us
    ppermute x3, starting transfers between devices, shards(): nx = lax.ppermute(x, 'lat', ring)  11 us
    ppermute x1, starting transfers between devices, shards(): lax.ppermute(weights, 'lat', swap)  8.79 us
    all_to_all x1, waiting for transfers between devices, spread(): return lax.all_to_all(copies, axis, 0, 0).reshape(-1, got.shape[2])  8.4 us
    all_to_all x2, waiting for transfers between devices, exchange(): lax.all_to_all(terms.reshape(n, terms.shape[0] // n, terms.shape[1]), axi...  7.99 us
  transfers between devices with their start and end apart: 18, of which 7 were waited for; matrix products, arithmetic and copies ran while one was open for 0% of the time, Pallas kernels for 12%

profile of v5, /device:TPU:1, one launch (start us, length us, event | category | flops | bytes accessed | tf_op | source)
XLA Modules:
  0.0 154.8 jit_solution(12602849496235001680)
XLA Ops:
  0.6 8.8 %collective-permute-start.1 = (bf16[256,4096]{1,0:T(8,128)(2,1)}, bf16[256,4096]{1,0:T(8,128)(2,1)S(1)}, u32[]{:S(2)}, u32[]{:S(2)}) collective-permute-start(bf16[256,4096]{1,0:T(8,128)(2,1)} %bitcast.10), channel_id=1, source_target_pairs={{0,32},{32,0},{64,96},{96,64},{128,160},{160,128},{192,224},{224,1... | collective-permute-start | bytes 6291464 | tf_op jit(solution)/shard_map/ppermute | solution.py:264
  9.4 5.3 %collective-permute-start = (bf16[1024,256]{1,0:T(8,128)(2,1)}, bf16[1024,256]{1,0:T(8,128)(2,1)}, u32[]{:S(2)}, u32[]{:S(2)}) collective-permute-start(bf16[1024,256]{1,0:T(8,128)(2,1)} %bitcast.18), channel_id=1, source_target_pairs={{0,64},{32,480},{64,128},{96,32},{128,192},{160,96},{192,256},{224... | collective-permute-start | bytes 1572872 | tf_op jit(solution)/shard_map/ppermute | solution.py:266
  23.3 4.9 %collective-permute-start.3 = (bf16[1024,256]{1,0:T(8,128)(2,1)}, bf16[1024,256]{1,0:T(8,128)(2,1)}, u32[]{:S(2)}, u32[]{:S(2)}) collective-permute-start(bf16[1024,256]{1,0:T(8,128)(2,1)} %collective-permute-done.refs_0_), channel_id=1, source_target_pairs={{0,64},{32,480},{64,128},{96,32},{128,192},{160,96},{192,256},{224... | collective-permute-start | bytes 1572872 | tf_op jit(solution)/shard_map/ppermute | solution.py:276
  28.2 5.3 %collective-permute-done.4.refs_1_ = bf16[1024,256]{1,0:T(8,128)(2,1)} collective-permute-done((bf16[1024,256]{1,0:T(8,128)(2,1)S(1)}, bf16[1024,256]{1,0:T(8,128)(2,1)}, u32[]{:S(2)}, u32[]{:S(2)}) %collective-permute-start.4) | collective-permute-done | bytes 524320 | tf_op jit(solution)/shard_map/ppermute | solution.py:265
  37.1 2.5 %shard_map.86 = (f32[1024,256]{1,0:T(8,128)S(1)}, bf16[512,256]{1,0:T(8,128)(2,1)S(1)}, f32[1024,256]{1,0:T(8,128)S(1)}, bf16[512,256]{1,0:T(8,128)(2,1)S(1)}) custom-call(s32[3]{0:T(128)S(1)} %pad_add_fusion.here, bf16[1024,256]{1,0:T(8,128)(2,1)} %collective-permute-done.refs_0_, bf16[1024,256]{1,0:T(8,128)(2,1)} %collective-permute-done.4.refs_1_, ...), custom_call_target="tpu_custom_call" | custom-call | flops 1000000000 | bytes 8912908 | tf_op jit(solution)/shard_map/pallas_call | solution.py:65
  39.7 2.3 %collective-permute-start.5 = (bf16[1024,256]{1,0:T(8,128)(2,1)}, bf16[1024,256]{1,0:T(8,128)(2,1)S(1)}, u32[]{:S(2)}, u32[]{:S(2)}) collective-permute-start(bf16[1024,256]{1,0:T(8,128)(2,1)} %collective-permute-done.3.refs_0_), channel_id=1, source_target_pairs={{0,64},{32,480},{64,128},{96,32},{128,192},{160,96},{192,256},{224... | collective-permute-start | bytes 1572872 | tf_op jit(solution)/shard_map/ppermute | solution.py:276
  44.0 4.5 %collective-permute-start.8 = (bf16[1024,256]{1,0:T(8,128)(2,1)}, bf16[1024,256]{1,0:T(8,128)(2,1)S(1)}, u32[]{:S(2)}, u32[]{:S(2)}) collective-permute-start(bf16[1024,256]{1,0:T(8,128)(2,1)} %collective-permute-done.6.refs_1_), channel_id=1, source_target_pairs={{0,64},{32,480},{64,128},{96,32},{128,192},{160,96},{192,256},{224... | collective-permute-start | bytes 1572872 | tf_op jit(solution)/shard_map/ppermute | solution.py:277
  48.5 2.5 %shard_map.87 = (f32[1024,256]{1,0:T(8,128)S(1)}, bf16[512,256]{1,0:T(8,128)(2,1)S(1)}, f32[1024,256]{1,0:T(8,128)S(1)}, bf16[512,256]{1,0:T(8,128)(2,1)S(1)}) custom-call(s32[3]{0:T(128)S(1)} %pad_add_fusion.here, bf16[1024,256]{1,0:T(8,128)(2,1)} %collective-permute-done.3.refs_0_, bf16[1024,256]{1,0:T(8,128)(2,1)} %collective-permute-done.6.refs_1_, ...), custom_call_target="tpu_custom_call" | custom-call | flops 1000000000 | bytes 11010060 | tf_op jit(solution)/shard_map/pallas_call | solution.py:65
  51.7 3.8 %collective-permute-start.7 = (bf16[1024,256]{1,0:T(8,128)(2,1)S(1)}, bf16[1024,256]{1,0:T(8,128)(2,1)S(1)}, u32[]{:S(2)}, u32[]{:S(2)}) collective-permute-start(bf16[1024,256]{1,0:T(8,128)(2,1)S(1)} %collective-permute-done.5.refs_0_), channel_id=1, source_target_pairs={{0,64},{32,480},{64,128},{96,32},{128,192},{160,96},{192,256},{224... | collective-permute-start | bytes 1572872 | tf_op jit(solution)/shard_map/ppermute | solution.py:276
  56.9 2.7 %shard_map.89 = (f32[1024,256]{1,0:T(8,128)S(1)}, bf16[512,256]{1,0:T(8,128)(2,1)S(1)}, f32[1024,256]{1,0:T(8,128)S(1)}, bf16[3,512,256]{2,1,0:T(8,128)(2,1)}) custom-call(s32[3]{0:T(128)S(1)} %pad_add_fusion.here, bf16[1024,256]{1,0:T(8,128)(2,1)S(1)} %collective-permute-done.5.refs_0_, bf16[1024,256]{1,0:T(8,128)(2,1)S(1)} %collective-permute-done.8.refs_1_, ...), custom_call_target="tpu_custom_call" | custom-call | flops 1000000000 | bytes 12058636 | tf_op jit(solution)/shard_map/pallas_call | solution.py:65
  59.6 3.7 %collective-permute-start.11 = (f32[1024,256]{1,0:T(8,128)S(1)}, f32[1024,256]{1,0:T(8,128)S(1)}, u32[]{:S(2)}, u32[]{:S(2)}) collective-permute-start(f32[1024,256]{1,0:T(8,128)S(1)} %get-tuple-element.58), channel_id=1, source_target_pairs={{0,32},{32,0},{64,96},{96,64},{128,160},{160,128},{192,224},{224,1... | collective-permute-start | bytes 3145736 | tf_op jit(solution)/shard_map/ppermute | solution.py:288
  63.4 3.2 %collective-permute-start.10 = (bf16[1024,256]{1,0:T(8,128)(2,1)S(1)}, bf16[1024,256]{1,0:T(8,128)(2,1)S(1)}, u32[]{:S(2)}, u32[]{:S(2)}) collective-permute-start(bf16[1024,256]{1,0:T(8,128)(2,1)S(1)} %collective-permute-done.7.ex), channel_id=1, source_target_pairs={{0,32},{32,0},{64,96},{96,64},{128,160},{160,128},{192,224},{224,1... | collective-permute-start | bytes 1572872 | tf_op jit(solution)/shard_map/ppermute | solution.py:291
  66.6 1.9 %collective-permute-start.12 = (bf16[3,512,256]{2,1,0:T(8,128)(2,1)}, bf16[3,512,256]{2,1,0:T(8,128)(2,1)}, u32[]{:S(2)}, u32[]{:S(2)}) collective-permute-start(bf16[3,512,256]{2,1,0:T(8,128)(2,1)} %get-tuple-element.60), channel_id=1, source_target_pairs={{0,32},{32,0},{64,96},{96,64},{128,160},{160,128},{192,224},{224,1... | collective-permute-start | bytes 2359304 | tf_op jit(solution)/shard_map/ppermute | solution.py:290
  70.5 7.9 %all-to-all-start = ((bf16[16,64,256]{2,1,0:T(8,128)(2,1)}), bf16[16,64,256]{2,1,0:T(8,128)(2,1)S(1)}, u32[]{:S(2)}, u32[]{:S(2)}) async-start(bf16[16,64,256]{2,1,0:T(8,128)(2,1)} %bitcast.6), calls=%async_computation | async-start | bytes 1048576 | tf_op jit(solution)/shard_map/all_to_all | solution.py:208
  86.1 5.5 %all-to-all-done.got = bf16[16,64,256]{2,1,0:T(8,128)(2,1)S(1)} async-done(((bf16[16,64,256]{2,1,0:T(8,128)(2,1)}), bf16[16,64,256]{2,1,0:T(8,128)(2,1)S(1)}, u32[]{:S(2)}, u32[]{:S(2)}) %all-to-all-start) | async-done | bytes 524320 | tf_op jit(solution)/shard_map/all_to_all | solution.py:208
  92.4 6.7 %all-to-all-start.1 = ((bf16[16,64,256]{2,1,0:T(8,128)(2,1)}), bf16[16,64,256]{2,1,0:T(8,128)(2,1)S(1)}, u32[]{:S(2)}, u32[]{:S(2)}) async-start(bf16[16,64,256]{2,1,0:T(8,128)(2,1)} %shard_map.92), calls=%async_computation.1 | async-start | bytes 1048576 | tf_op jit(solution)/shard_map/all_to_all | solution.py:218
  99.1 4.4 %collective-permute-start.13 = (bf16[4,512,256]{2,1,0:T(8,128)(2,1)S(1)}, bf16[4,512,256]{2,1,0:T(8,128)(2,1)}, u32[]{:S(2)}, u32[]{:S(2)}) collective-permute-start(bf16[4,512,256]{2,1,0:T(8,128)(2,1)S(1)} %copy-done.12), channel_id=1, source_target_pairs={{0,1},{1,0},{2,3},{3,2},{4,5},{5,4},{6,7},{7,6},{8,9},{9,8},{10,11... | collective-permute-start | bytes 3145736 | tf_op jit(solution)/shard_map/ppermute | solution.py:297
  103.5 8.4 %all-to-all-done.1 = bf16[16,64,256]{2,1,0:T(8,128)(2,1)S(1)} async-done(((bf16[16,64,256]{2,1,0:T(8,128)(2,1)}), bf16[16,64,256]{2,1,0:T(8,128)(2,1)S(1)}, u32[]{:S(2)}, u32[]{:S(2)}) %all-to-all-start.1) | async-done | bytes 524320 | tf_op jit(solution)/shard_map/all_to_all | solution.py:218
  113.0 6.9 %all-to-all-start.2 = ((bf16[16,64,256]{2,1,0:T(8,128)(2,1)}), bf16[16,64,256]{2,1,0:T(8,128)(2,1)S(1)}, u32[]{:S(2)}, u32[]{:S(2)}) async-start(bf16[16,64,256]{2,1,0:T(8,128)(2,1)} %bitcast.8), calls=%async_computation.2 | async-start | bytes 1048576 | tf_op jit(solution)/shard_map/all_to_all | solution.py:208
  120.8 4.4 %collective-permute-start.14 = (f32[128,256]{1,0:T(8,128)S(1)}, f32[128,256]{1,0:T(8,128)S(1)}, u32[]{:S(2)}, u32[]{:S(2)}) collective-permute-start(f32[128,256]{1,0:T(8,128)S(1)} %get-tuple-element.71), channel_id=1, source_target_pairs={{0,1},{1,0},{2,3},{3,2},{4,5},{5,4},{6,7},{7,6},{8,9},{9,8},{10,11... | collective-permute-start | bytes 393224 | tf_op jit(solution)/shard_map/ppermute | solution.py:302
  125.2 6.2 %collective-permute-done.13.other = bf16[4,512,256]{2,1,0:T(8,128)(2,1)} collective-permute-done((bf16[4,512,256]{2,1,0:T(8,128)(2,1)S(1)}, bf16[4,512,256]{2,1,0:T(8,128)(2,1)}, u32[]{:S(2)}, u32[]{:S(2)}) %collective-permute-start.13) | collective-permute-done | bytes 1048608 | tf_op jit(solution)/shard_map/ppermute | solution.py:297
  131.4 2.5 %shard_map.94 = bf16[256,2048]{1,0:T(8,128)(2,1)} custom-call(s32[3]{0:T(128)S(1)} %pad_add_fusion.here, bf16[4,512,256]{2,1,0:T(8,128)(2,1)S(1)} %copy-done.23, bf16[4,512,256]{2,1,0:T(8,128)(2,1)} %collective-permute-done.13.other), custom_call_target="tpu_custom_call" | custom-call | flops 2000000000 | bytes 3145740 | tf_op jit(solution)/shard_map/pallas_call | solution.py:65
  134.7 2.5 %all-to-all-done.2.got = bf16[16,64,256]{2,1,0:T(8,128)(2,1)S(1)} async-done(((bf16[16,64,256]{2,1,0:T(8,128)(2,1)}), bf16[16,64,256]{2,1,0:T(8,128)(2,1)S(1)}, u32[]{:S(2)}, u32[]{:S(2)}) %all-to-all-start.2) | async-done | bytes 524320 | tf_op jit(solution)/shard_map/all_to_all | solution.py:208
  137.3 16.7 %all_gather.3 = bf16[1024,256]{1,0:T(8,128)(2,1)S(1)} all-gather(bf16[64,256]{1,0:T(8,128)(2,1)S(1)} %shard_map.96), channel_id=1, replica_groups=mesh['lat'=16,'tgt'=16,'tok'=2] {'lat'}, dimensions={0}, use_global_device_ids=true | all-gather | bytes 557056 | tf_op jit(solution)/shard_map/all_gather | solution.py:306
  (76 shorter events, 30.3 us)
Async XLA Ops:
  0.6 21.3 %collective-permute-start.1 = (bf16[256,4096]{1,0:T(8,128)(2,1)}, bf16[256,4096]{1,0:T(8,128)(2,1)S(1)}, u32[]{:S(2)}, u32[]{:S(2)}) collective-permute-start(bf16[256,4096]{1,0:T(8,128)(2,1)} %bitcast.10), channel_id=1, source_target_pairs={{0,32},{32,0},{64,96},{96,64},{128,160},{160,128},{192,224},{224,1... | collective-permute-start | bytes 6291464 | tf_op jit(solution)/shard_map/ppermute | solution.py:264
  9.4 12.5 %collective-permute-start = (bf16[1024,256]{1,0:T(8,128)(2,1)}, bf16[1024,256]{1,0:T(8,128)(2,1)}, u32[]{:S(2)}, u32[]{:S(2)}) collective-permute-start(bf16[1024,256]{1,0:T(8,128)(2,1)} %bitcast.18), channel_id=1, source_target_pairs={{0,64},{32,480},{64,128},{96,32},{128,192},{160,96},{192,256},{224... | collective-permute-start | bytes 1572872 | tf_op jit(solution)/shard_map/ppermute | solution.py:266
  16.5 19.1 %copy-start = (bf16[1,256,4096]{2,1,0:T(8,128)(2,1)S(1)}, bf16[1,256,4096]{2,1,0:T(8,128)(2,1)}, u32[]{:S(2)}) copy-start(bf16[1,256,4096]{2,1,0:T(8,128)(2,1)} %param.7) | copy-start | bytes 6291460
  18.1 3.9 %collective-permute-start.2 = (bf16[256,1024]{1,0:T(8,128)(2,1)S(1)}, bf16[256,1024]{1,0:T(8,128)(2,1)S(1)}, u32[]{:S(2)}, u32[]{:S(2)}) collective-permute-start(bf16[256,1024]{1,0:T(8,128)(2,1)S(1)} %get-tuple-element.38.refs_3_.lat_t), channel_id=1, source_target_pairs={{0,32},{32,0},{64,96},{96,64},{128,160},{160,128},{192,224},{224,1... | collective-permute-start | bytes 1572872 | tf_op jit(solution)/shard_map/ppermute | solution.py:264
  20.0 13.5 %collective-permute-start.4 = (bf16[1024,256]{1,0:T(8,128)(2,1)S(1)}, bf16[1024,256]{1,0:T(8,128)(2,1)}, u32[]{:S(2)}, u32[]{:S(2)}) collective-permute-start(bf16[1024,256]{1,0:T(8,128)(2,1)S(1)} %bitcast.19), channel_id=1, source_target_pairs={{0,480},{32,64},{64,32},{96,128},{128,96},{160,192},{192,160},{224... | collective-permute-start | bytes 1572872 | tf_op jit(solution)/shard_map/ppermute | solution.py:265
  23.3 16.4 %collective-permute-start.3 = (bf16[1024,256]{1,0:T(8,128)(2,1)}, bf16[1024,256]{1,0:T(8,128)(2,1)}, u32[]{:S(2)}, u32[]{:S(2)}) collective-permute-start(bf16[1024,256]{1,0:T(8,128)(2,1)} %collective-permute-done.refs_0_), channel_id=1, source_target_pairs={{0,64},{32,480},{64,128},{96,32},{128,192},{160,96},{192,256},{224... | collective-permute-start | bytes 1572872 | tf_op jit(solution)/shard_map/ppermute | solution.py:276
  33.5 10.5 %collective-permute-start.6 = (bf16[1024,256]{1,0:T(8,128)(2,1)}, bf16[1024,256]{1,0:T(8,128)(2,1)}, u32[]{:S(2)}, u32[]{:S(2)}) collective-permute-start(bf16[1024,256]{1,0:T(8,128)(2,1)} %collective-permute-done.4.refs_1_), channel_id=1, source_target_pairs={{0,64},{32,480},{64,128},{96,32},{128,192},{160,96},{192,256},{224... | collective-permute-start | bytes 1572872 | tf_op jit(solution)/shard_map/ppermute | solution.py:277
  39.7 12.1 %collective-permute-start.5 = (bf16[1024,256]{1,0:T(8,128)(2,1)}, bf16[1024,256]{1,0:T(8,128)(2,1)S(1)}, u32[]{:S(2)}, u32[]{:S(2)}) collective-permute-start(bf16[1024,256]{1,0:T(8,128)(2,1)} %collective-permute-done.3.refs_0_), channel_id=1, source_target_pairs={{0,64},{32,480},{64,128},{96,32},{128,192},{160,96},{192,256},{224... | collective-permute-start | bytes 1572872 | tf_op jit(solution)/shard_map/ppermute | solution.py:276
  42.0 13.5 %collective-permute-start.9 = (bf16[1024,256]{1,0:T(8,128)(2,1)S(1)}, bf16[1024,256]{1,0:T(8,128)(2,1)S(1)}, u32[]{:S(2)}, u32[]{:S(2)}) collective-permute-start(bf16[1024,256]{1,0:T(8,128)(2,1)S(1)} %bitcast.20), channel_id=1, source_target_pairs={{0,32},{32,0},{64,96},{96,64},{128,160},{160,128},{192,224},{224,1... | collective-permute-start | bytes 1572872 | tf_op jit(solution)/shard_map/ppermute | solution.py:273
  44.0 12.8 %collective-permute-start.8 = (bf16[1024,256]{1,0:T(8,128)(2,1)}, bf16[1024,256]{1,0:T(8,128)(2,1)S(1)}, u32[]{:S(2)}, u32[]{:S(2)}) collective-permute-start(bf16[1024,256]{1,0:T(8,128)(2,1)} %collective-permute-done.6.refs_1_), channel_id=1, source_target_pairs={{0,64},{32,480},{64,128},{96,32},{128,192},{160,96},{192,256},{224... | collective-permute-start | bytes 1572872 | tf_op jit(solution)/shard_map/ppermute | solution.py:277
  51.7 11.6 %collective-permute-start.7 = (bf16[1024,256]{1,0:T(8,128)(2,1)S(1)}, bf16[1024,256]{1,0:T(8,128)(2,1)S(1)}, u32[]{:S(2)}, u32[]{:S(2)}) collective-permute-start(bf16[1024,256]{1,0:T(8,128)(2,1)S(1)} %collective-permute-done.5.refs_0_), channel_id=1, source_target_pairs={{0,64},{32,480},{64,128},{96,32},{128,192},{160,96},{192,256},{224... | collective-permute-start | bytes 1572872 | tf_op jit(solution)/shard_map/ppermute | solution.py:276
  56.8 11.7 %copy-start.7 = (bf16[1024,256]{1,0:T(8,128)(2,1)S(1)}, bf16[1024,256]{1,0:T(8,128)(2,1)}, u32[]{:S(2)}) copy-start(bf16[1024,256]{1,0:T(8,128)(2,1)} %copy-done.6) | copy-start | bytes 1572868
  59.6 10.9 %copy-start.19 = (bf16[512,256]{1,0:T(8,128)(2,1)}, bf16[512,256]{1,0:T(8,128)(2,1)S(1)}, u32[]{:S(2)}) copy-start(bf16[512,256]{1,0:T(8,128)(2,1)S(1)} %get-tuple-element.64.refs_3_) | copy-start | bytes 786436
  59.6 9.0 %collective-permute-start.11 = (f32[1024,256]{1,0:T(8,128)S(1)}, f32[1024,256]{1,0:T(8,128)S(1)}, u32[]{:S(2)}, u32[]{:S(2)}) collective-permute-start(f32[1024,256]{1,0:T(8,128)S(1)} %get-tuple-element.58), channel_id=1, source_target_pairs={{0,32},{32,0},{64,96},{96,64},{128,160},{160,128},{192,224},{224,1... | collective-permute-start | bytes 3145736 | tf_op jit(solution)/shard_map/ppermute | solution.py:288
  63.4 5.2 %collective-permute-start.10 = (bf16[1024,256]{1,0:T(8,128)(2,1)S(1)}, bf16[1024,256]{1,0:T(8,128)(2,1)S(1)}, u32[]{:S(2)}, u32[]{:S(2)}) collective-permute-start(bf16[1024,256]{1,0:T(8,128)(2,1)S(1)} %collective-permute-done.7.ex), channel_id=1, source_target_pairs={{0,32},{32,0},{64,96},{96,64},{128,160},{160,128},{192,224},{224,1... | collective-permute-start | bytes 1572872 | tf_op jit(solution)/shard_map/ppermute | solution.py:291
  66.6 11.7 %collective-permute-start.12 = (bf16[3,512,256]{2,1,0:T(8,128)(2,1)}, bf16[3,512,256]{2,1,0:T(8,128)(2,1)}, u32[]{:S(2)}, u32[]{:S(2)}) collective-permute-start(bf16[3,512,256]{2,1,0:T(8,128)(2,1)} %get-tuple-element.60), channel_id=1, source_target_pairs={{0,32},{32,0},{64,96},{96,64},{128,160},{160,128},{192,224},{224,1... | collective-permute-start | bytes 2359304 | tf_op jit(solution)/shard_map/ppermute | solution.py:290
  70.5 21.1 %all-to-all-start = ((bf16[16,64,256]{2,1,0:T(8,128)(2,1)}), bf16[16,64,256]{2,1,0:T(8,128)(2,1)S(1)}, u32[]{:S(2)}, u32[]{:S(2)}) async-start(bf16[16,64,256]{2,1,0:T(8,128)(2,1)} %bitcast.6), calls=%async_computation | async-start | bytes 1048576 | tf_op jit(solution)/shard_map/all_to_all | solution.py:208
  86.1 25.8 %copy-start.10 = (bf16[256,256]{1,0:T(8,128)(2,1)S(1)}, bf16[256,256]{1,0:T(8,128)(2,1)}, u32[]{:S(2)}) copy-start(bf16[256,256]{1,0:T(8,128)(2,1)} %encoder.1) | copy-start | bytes 393220
  91.6 28.4 %copy-start.14 = (bf16[1024,256]{1,0:T(8,128)(2,1)S(1)}, bf16[1024,256]{1,0:T(8,128)(2,1)}, u32[]{:S(2)}) copy-start(bf16[1024,256]{1,0:T(8,128)(2,1)} %inputs.1) | copy-start | bytes 1572868
  92.4 19.5 %all-to-all-start.1 = ((bf16[16,64,256]{2,1,0:T(8,128)(2,1)}), bf16[16,64,256]{2,1,0:T(8,128)(2,1)S(1)}, u32[]{:S(2)}, u32[]{:S(2)}) async-start(bf16[16,64,256]{2,1,0:T(8,128)(2,1)} %shard_map.92), calls=%async_computation.1 | async-start | bytes 1048576 | tf_op jit(solution)/shard_map/all_to_all | solution.py:218
  99.1 32.2 %collective-permute-start.13 = (bf16[4,512,256]{2,1,0:T(8,128)(2,1)S(1)}, bf16[4,512,256]{2,1,0:T(8,128)(2,1)}, u32[]{:S(2)}, u32[]{:S(2)}) collective-permute-start(bf16[4,512,256]{2,1,0:T(8,128)(2,1)S(1)} %copy-done.12), channel_id=1, source_target_pairs={{0,1},{1,0},{2,3},{3,2},{4,5},{5,4},{6,7},{7,6},{8,9},{9,8},{10,11... | collective-permute-start | bytes 3145736 | tf_op jit(solution)/shard_map/ppermute | solution.py:297
  113.0 24.2 %all-to-all-start.2 = ((bf16[16,64,256]{2,1,0:T(8,128)(2,1)}), bf16[16,64,256]{2,1,0:T(8,128)(2,1)S(1)}, u32[]{:S(2)}, u32[]{:S(2)}) async-start(bf16[16,64,256]{2,1,0:T(8,128)(2,1)} %bitcast.8), calls=%async_computation.2 | async-start | bytes 1048576 | tf_op jit(solution)/shard_map/all_to_all | solution.py:208
  119.9 11.5 %copy-start.23 = (bf16[4,512,256]{2,1,0:T(8,128)(2,1)S(1)}, bf16[4,512,256]{2,1,0:T(8,128)(2,1)}, u32[]{:S(2)}) copy-start(bf16[4,512,256]{2,1,0:T(8,128)(2,1)} %copy-done.22) | copy-start | bytes 3145732
  120.8 13.2 %collective-permute-start.14 = (f32[128,256]{1,0:T(8,128)S(1)}, f32[128,256]{1,0:T(8,128)S(1)}, u32[]{:S(2)}, u32[]{:S(2)}) collective-permute-start(f32[128,256]{1,0:T(8,128)S(1)} %get-tuple-element.71), channel_id=1, source_target_pairs={{0,1},{1,0},{2,3},{3,2},{4,5},{5,4},{6,7},{7,6},{8,9},{9,8},{10,11... | collective-permute-start | bytes 393224 | tf_op jit(solution)/shard_map/ppermute | solution.py:302
  (18 other events, 43.0 us)
